TPU v7x, 32 devices: a whole 2x2x4 slice. The times are simulated.
32 devices in a mesh: ctx: 32 (over z, y, x, core).
Axes of the slice: x: 2, y: 2, z: 4, core: 2. Of those that a mesh axis runs over, the one named last changes fastest.
Arguments:
- hidden_in: bfloat16 [4096, 576], P('ctx'), may hold values from -6 to 6
- attention_gain: float32 [576], replicated, may hold values from 0.5 to 1.5
- query_weight: bfloat16 [32, 10368], P('ctx'), may hold values from -0.25 to 0.25
- key_weight: bfloat16 [32, 3456], P('ctx'), may hold values from -0.25 to 0.25
- value_weight: bfloat16 [32, 3456], P('ctx'), may hold values from -0.25 to 0.25
- output_weight: bfloat16 [32, 10368], P('ctx'), may hold values from -2 to 2
- feedforward_gain: float32 [576], replicated, may hold values from 0.5 to 1.5
- gate_weight: bfloat16 [32, 27648], P('ctx'), may hold values from -0.25 to 0.25
- up_weight: bfloat16 [32, 27648], P('ctx'), may hold values from -0.25 to 0.25
- down_weight: bfloat16 [32, 27648], P('ctx'), may hold values from -0.15625 to 0.15625
- doc_of_block: int32 [64], replicated, may hold values from 0 to 1, as said below
- pair_table: int32 [32], replicated, may hold values from 0 to 31, each once
- out_grad: bfloat16 [4096, 576], P('ctx'), may hold values from -6 to 6
Outputs:
- block_out: bfloat16 [4096, 576], P('ctx')
- input_grad: bfloat16 [4096, 576], P('ctx')
- attention_gain_grad: float32 [576], replicated
- query_weight_grad: float32 [32, 10368], P('ctx')
- key_weight_grad: float32 [32, 3456], P('ctx')
- value_weight_grad: float32 [32, 3456], P('ctx')
- output_weight_grad: float32 [32, 10368], P('ctx')
- feedforward_gain_grad: float32 [576], replicated
- gate_weight_grad: float32 [32, 27648], P('ctx')
- up_weight_grad: float32 [32, 27648], P('ctx')
- down_weight_grad: float32 [32, 27648], P('ctx')
Inputs may be any that keep to these rules, and one draw needn't show every extreme that they name: `doc_of_block`: never falling along the stream, rising by at most one from block to block; document 0 starts at block 0 and holds 32 to 40 blocks; every document holds max(1, 16) blocks or more. `pair_table`: each value once.
All inputs are finite; a program needn't handle non-finite values.
Results may differ from a plain program's by a relative error of at most 0.025.
Values may be sent and summed in bfloat16 or wider, within the bound.
No kernel may reach another device: no remote copies, remote signals or barrier semaphores. Data moves between devices by JAX's collectives and lax.ppermute only.
A program may use at most 192 MiB of HBM per device.

v0:
```python
import math

import jax
import jax.numpy as jnp
from jax import lax
from jax.sharding import PartitionSpec as P

HEADS = 9
KV_HEADS = 3
HEAD_SIZE = 64


epsilon = 1e-05
rope_base = 100000.0
masked_score = -1e30
key_block = 2048


def token_layout(doc_of_block, pair_table, half_rows):
    pair_count = pair_table.shape[0]
    block_total = 2 * pair_count
    stored = jnp.arange(block_total, dtype=jnp.int32)
    owner = stored // 2
    pair_iota = jnp.arange(pair_count, dtype=jnp.int32)
    pair_of = jnp.sum(
        jnp.where(owner[:, None] == pair_iota[None, :], pair_table[None, :], 0), axis=1
    )
    stream_block = jnp.where(stored % 2 == 0, pair_of, block_total - 1 - pair_of)
    block_iota = jnp.arange(block_total, dtype=jnp.int32)
    doc_stored = jnp.sum(
        jnp.where(stream_block[:, None] == block_iota[None, :], doc_of_block[None, :], 0), axis=1
    )
    same_doc = doc_stored[:, None] == doc_of_block[None, :]
    doc_start = jnp.min(jnp.where(same_doc, block_iota[None, :], block_total), axis=1)
    offsets = jnp.arange(half_rows, dtype=jnp.int32)
    stream_index = (stream_block[:, None] * half_rows + offsets[None, :]).reshape(-1)
    position = ((stream_block - doc_start)[:, None] * half_rows + offsets[None, :]).reshape(-1)
    document = jnp.broadcast_to(doc_stored[:, None], (block_total, half_rows)).reshape(-1)
    return (document, stream_index, position)


def rotary(values, positions, direction):
    row_count = values.shape[0]
    head_count = values.shape[1] // HEAD_SIZE
    half_dim = HEAD_SIZE // 2
    shaped = values.reshape(row_count, head_count, HEAD_SIZE)
    frequency = rope_base ** (-jnp.arange(half_dim, dtype=jnp.float32) * (2.0 / HEAD_SIZE))
    angles = positions.astype(jnp.float32)[:, None] * frequency[None, :]
    cosine = jnp.cos(angles)[:, None, :]
    sine = direction * jnp.sin(angles)[:, None, :]
    leading = shaped[..., :half_dim]
    trailing = shaped[..., half_dim:]
    turned = jnp.concatenate(
        [leading * cosine - trailing * sine, trailing * cosine + leading * sine], axis=-1
    )
    return turned.reshape(row_count, head_count * HEAD_SIZE)


def norm_rows(values, gain):
    inverse = lax.rsqrt(jnp.mean(values * values, axis=-1, keepdims=True) + epsilon)
    return values * inverse * gain


def norm_back(values, gain, grad):
    inverse = lax.rsqrt(jnp.mean(values * values, axis=-1, keepdims=True) + epsilon)
    unit = values * inverse
    scaled = grad * gain
    gain_part = jnp.sum(grad * unit, axis=0)
    input_part = inverse * (scaled - unit * jnp.mean(scaled * unit, axis=-1, keepdims=True))
    return (input_part, gain_part)


def visible(query_doc, query_index, key_doc, key_index):
    return (query_doc[:, None] == key_doc[None, :]) & (key_index[None, :] <= query_index[:, None])


def fold_blocks(advance_block, carried, arrays):
    length = arrays[0].shape[0]
    width = math.gcd(length, key_block)
    block_count = length // width
    stacked = tuple((item.reshape((block_count, width) + item.shape[1:]) for item in arrays))
    block_starts = width * jnp.arange(block_count, dtype=jnp.int32)

    def advance(running, inputs):
        return (advance_block(running, inputs[0], inputs[1]), None)

    return lax.scan(advance, carried, (stacked, block_starts))[0]


def forward_block(carried, query_rot, key_rot, value_low, allowed):
    total, run_max, run_sum = carried
    query_count = query_rot.shape[0]
    group_count = HEADS // KV_HEADS
    grouped_heads = query_rot.reshape(query_count, KV_HEADS, group_count, HEAD_SIZE)
    head_keys = key_rot.reshape(-1, KV_HEADS, HEAD_SIZE)
    head_values = value_low.reshape(-1, KV_HEADS, HEAD_SIZE)
    attention_scores = jnp.einsum(
        "fiam,pim->iafp", grouped_heads, head_keys, preferred_element_type=jnp.float32
    ) * HEAD_SIZE ** (-0.5)
    masked = jnp.where(allowed, attention_scores, masked_score)
    new_max = jnp.maximum(run_max, jnp.max(masked, axis=-1))
    weights = jnp.where(allowed, jnp.exp(masked - new_max[..., None]), 0.0)
    factor = jnp.exp(run_max - new_max)
    total = total * factor[..., None] + jnp.einsum(
        "vykm,mvx->vykx",
        weights.astype(jnp.bfloat16),
        head_values,
        preferred_element_type=jnp.float32,
    )
    run_sum = run_sum * factor + jnp.sum(weights, axis=-1)
    return (total, new_max, run_sum)


def backward_terms(query_rot, grad_low, log_total, delta, key_rot, value_low, allowed):
    query_count = query_rot.shape[0]
    key_count = key_rot.shape[0]
    group_count = HEADS // KV_HEADS
    scale_factor = HEAD_SIZE ** (-0.5)
    grouped_heads = query_rot.reshape(query_count, KV_HEADS, group_count, HEAD_SIZE)
    head_gradient_rows = grad_low.reshape(query_count, KV_HEADS, group_count, HEAD_SIZE)
    head_keys = key_rot.reshape(key_count, KV_HEADS, HEAD_SIZE)
    head_values = value_low.reshape(key_count, KV_HEADS, HEAD_SIZE)
    attention_scores = (
        jnp.einsum("fiam,pim->iafp", grouped_heads, head_keys, preferred_element_type=jnp.float32)
        * scale_factor
    )
    attention_probability = jnp.where(
        allowed, jnp.exp(attention_scores - log_total[..., None]), 0.0
    )
    grad_probs = jnp.einsum(
        "fiam,pim->iafp", head_gradient_rows, head_values, preferred_element_type=jnp.float32
    )
    score_gradient = (attention_probability * (grad_probs - delta[..., None])).astype(jnp.bfloat16)
    query_part = (
        jnp.einsum("vykm,mvx->vykx", score_gradient, head_keys, preferred_element_type=jnp.float32)
        * scale_factor
    )
    key_part = (
        jnp.einsum(
            "yohx,hyol->xyl", score_gradient, grouped_heads, preferred_element_type=jnp.float32
        )
        * scale_factor
    )
    value_part = jnp.einsum(
        "yohx,hyol->xyl",
        attention_probability.astype(jnp.bfloat16),
        head_gradient_rows,
        preferred_element_type=jnp.float32,
    )
    return (query_part, key_part.reshape(key_count, -1), value_part.reshape(key_count, -1))


def left_product(left, right):
    return jnp.einsum("td,tf->df", left, right, preferred_element_type=jnp.float32)


def right_product(grad, weight):
    return jnp.einsum("tf,df->td", grad, weight, preferred_element_type=jnp.float32)


def body(
    hidden_in,
    attention_gain,
    query_weight,
    key_weight,
    value_weight,
    output_weight,
    feedforward_gain,
    gate_weight,
    up_weight,
    down_weight,
    doc_of_block,
    pair_table,
    out_grad,
):
    local_rows = hidden_in.shape[0]
    model_width = hidden_in.shape[1]
    group_count = HEADS // KV_HEADS
    device = lax.axis_index("ctx")
    document_all, stream_all, position_all = token_layout(doc_of_block, pair_table, local_rows // 2)
    own_start = device * local_rows
    own_doc = lax.dynamic_slice_in_dim(document_all, own_start, local_rows)
    own_stream = lax.dynamic_slice_in_dim(stream_all, own_start, local_rows)
    own_position = lax.dynamic_slice_in_dim(position_all, own_start, local_rows)
    gathered = (
        lax.all_gather(query_weight, "ctx", axis=0, tiled=True),
        lax.all_gather(key_weight, "ctx", axis=0, tiled=True),
        lax.all_gather(value_weight, "ctx", axis=0, tiled=True),
        lax.all_gather(output_weight, "ctx", axis=0, tiled=True),
        lax.all_gather(gate_weight, "ctx", axis=0, tiled=True),
        lax.all_gather(up_weight, "ctx", axis=0, tiled=True),
        lax.all_gather(down_weight, "ctx", axis=0, tiled=True),
    )
    query_full = gathered[0].reshape(model_width, model_width)
    key_full = gathered[1].reshape(model_width, -1)
    value_full = gathered[2].reshape(model_width, -1)
    output_full = gathered[3].reshape(model_width, model_width)
    gate_full = gathered[4].reshape(model_width, -1)
    up_full = gathered[5].reshape(model_width, -1)
    down_full = gathered[6].reshape(-1, model_width)
    hidden_f = hidden_in.astype(jnp.float32)
    normed = norm_rows(hidden_f, attention_gain).astype(jnp.bfloat16)
    query_pre = jnp.dot(normed, query_full, preferred_element_type=jnp.float32)
    key_pre = jnp.dot(normed, key_full, preferred_element_type=jnp.float32)
    value_low = jnp.dot(normed, value_full, preferred_element_type=jnp.float32).astype(jnp.bfloat16)
    query_rot = rotary(query_pre, own_position, 1.0).astype(jnp.bfloat16)
    key_rot = rotary(key_pre, own_position, 1.0).astype(jnp.bfloat16)
    head_shape = (KV_HEADS, group_count, local_rows)
    start_state = (
        jnp.zeros(head_shape + (HEAD_SIZE,), jnp.float32),
        jnp.full(head_shape, masked_score, jnp.float32),
        jnp.zeros(head_shape, jnp.float32),
    )
    shard_rows = (
        lax.all_gather(key_rot, "ctx", axis=0, tiled=True),
        lax.all_gather(value_low, "ctx", axis=0, tiled=True),
    )
    key_doc = document_all
    key_stream = stream_all

    def advance_block(running, block_data, block_first):
        allowed = visible(own_doc, own_stream, block_data[2], block_data[3])

        def update():
            return forward_block(running, query_rot, block_data[0], block_data[1], allowed)

        return update()

    total, run_max, run_sum = fold_blocks(
        advance_block, start_state, (shard_rows[0], shard_rows[1], key_doc, key_stream)
    )
    attention = total / run_sum[..., None]
    log_total = run_max + jnp.log(run_sum)
    attended = attention.transpose(2, 0, 1, 3).reshape(local_rows, model_width).astype(jnp.bfloat16)
    middle = hidden_f + jnp.dot(attended, output_full, preferred_element_type=jnp.float32)
    normed_two = norm_rows(middle, feedforward_gain).astype(jnp.bfloat16)
    gate_act = jnp.dot(normed_two, gate_full, preferred_element_type=jnp.float32)
    up_act = jnp.dot(normed_two, up_full, preferred_element_type=jnp.float32)
    sigma = jax.nn.sigmoid(gate_act)
    silu_gate = gate_act * sigma
    hidden_ff = (silu_gate * up_act).astype(jnp.bfloat16)
    block_out = (middle + jnp.dot(hidden_ff, down_full, preferred_element_type=jnp.float32)).astype(
        jnp.bfloat16
    )
    down_grad = left_product(hidden_ff, out_grad)
    grad_inner = right_product(out_grad, down_full)
    grad_gate = (grad_inner * up_act * sigma * (1.0 + gate_act * (1.0 - sigma))).astype(
        jnp.bfloat16
    )
    grad_up = (grad_inner * silu_gate).astype(jnp.bfloat16)
    gate_grad = left_product(normed_two, grad_gate)
    up_grad = left_product(normed_two, grad_up)
    grad_normed_two = right_product(grad_gate, gate_full) + right_product(grad_up, up_full)
    middle_part, second_gain_part = norm_back(middle, feedforward_gain, grad_normed_two)
    grad_middle = out_grad.astype(jnp.float32) + middle_part
    grad_branch = grad_middle.astype(jnp.bfloat16)
    output_grad_w = left_product(attended, grad_branch)
    grad_low = right_product(grad_branch, output_full).astype(jnp.bfloat16)
    head_gradient_rows = (
        grad_low.reshape(local_rows, KV_HEADS, group_count, HEAD_SIZE)
        .transpose(1, 2, 0, 3)
        .astype(jnp.float32)
    )
    delta = jnp.sum(head_gradient_rows * attention, axis=-1)
    kv_width = key_rot.shape[1]
    back_state = (
        jnp.zeros(head_shape + (HEAD_SIZE,), jnp.float32),
        jnp.zeros((local_rows * lax.axis_size("ctx"), 2 * kv_width), jnp.float32),
    )
    shard_rows = (
        lax.all_gather(key_rot, "ctx", axis=0, tiled=True),
        lax.all_gather(value_low, "ctx", axis=0, tiled=True),
    )
    key_doc = document_all
    key_stream = stream_all

    def advance_block(running, block_data, block_first):
        allowed = visible(own_doc, own_stream, block_data[2], block_data[3])

        def update():
            query_part, key_part, value_part = backward_terms(
                query_rot, grad_low, log_total, delta, block_data[0], block_data[1], allowed
            )
            joined = jnp.concatenate([key_part, value_part], axis=1)
            return (
                running[0] + query_part,
                lax.dynamic_update_slice_in_dim(running[1], joined, block_first, 0),
            )

        return update()

    grad_query_heads, partial_kv = fold_blocks(
        advance_block, back_state, (shard_rows[0], shard_rows[1], key_doc, key_stream)
    )
    own_kv = lax.psum_scatter(partial_kv, "ctx", scatter_dimension=0, tiled=True)
    grad_key_rot = own_kv[:, :kv_width]
    grad_value = own_kv[:, kv_width:]
    grad_query_rot = grad_query_heads.transpose(2, 0, 1, 3).reshape(local_rows, model_width)
    grad_query = rotary(grad_query_rot, own_position, -1.0).astype(jnp.bfloat16)
    grad_key = rotary(grad_key_rot, own_position, -1.0).astype(jnp.bfloat16)
    grad_value_low = grad_value.astype(jnp.bfloat16)
    query_grad = left_product(normed, grad_query)
    key_grad = left_product(normed, grad_key)
    value_grad = left_product(normed, grad_value_low)
    grad_normed = (
        right_product(grad_query, query_full)
        + right_product(grad_key, key_full)
        + right_product(grad_value_low, value_full)
    )
    input_part, first_gain_part = norm_back(hidden_f, attention_gain, grad_normed)
    input_grad = (grad_middle + input_part).astype(jnp.bfloat16)
    device_count = lax.axis_size("ctx")
    summed = (
        lax.psum_scatter(
            query_grad.reshape(device_count, -1), "ctx", scatter_dimension=0, tiled=True
        ),
        lax.psum_scatter(
            key_grad.reshape(device_count, -1), "ctx", scatter_dimension=0, tiled=True
        ),
        lax.psum_scatter(
            value_grad.reshape(device_count, -1), "ctx", scatter_dimension=0, tiled=True
        ),
        lax.psum_scatter(
            output_grad_w.reshape(device_count, -1), "ctx", scatter_dimension=0, tiled=True
        ),
        lax.psum_scatter(
            gate_grad.reshape(device_count, -1), "ctx", scatter_dimension=0, tiled=True
        ),
        lax.psum_scatter(up_grad.reshape(device_count, -1), "ctx", scatter_dimension=0, tiled=True),
        lax.psum_scatter(
            down_grad.reshape(device_count, -1), "ctx", scatter_dimension=0, tiled=True
        ),
    )
    gain_one, gain_two = lax.psum((first_gain_part, second_gain_part), "ctx")
    return (
        block_out,
        input_grad,
        gain_one,
        summed[0],
        summed[1],
        summed[2],
        summed[3],
        gain_two,
        summed[4],
        summed[5],
        summed[6],
    )


def solution(mesh):
    in_specs = (
        P("ctx", None),
        P(),
        P("ctx", None),
        P("ctx", None),
        P("ctx", None),
        P("ctx", None),
        P(),
        P("ctx", None),
        P("ctx", None),
        P("ctx", None),
        P(),
        P(),
        P("ctx", None),
    )
    out_specs = (
        P("ctx", None),
        P("ctx", None),
        P(),
        P("ctx", None),
        P("ctx", None),
        P("ctx", None),
        P("ctx", None),
        P(),
        P("ctx", None),
        P("ctx", None),
        P("ctx", None),
    )
    return jax.shard_map(body, mesh=mesh, in_specs=in_specs, out_specs=out_specs, check_vma=False)
```

profile of v0, /device:TPU:0, one launch (start us, length us, event | category | flops | bytes accessed | tf_op | source)
XLA Modules:
  0.0 869.9 jit_solution(8195260370932170851)
XLA Ops:
  8.0 44.7 %all-gather = bf16[32,1,3456]{2,1,0:T(2,128)(2,1)S(1)} all-gather(bf16[1,1,3456]{2,1,0:T(2,128)(2,1)} %bitcast.261), channel_id=1, replica_groups=mesh['ctx'=32] {'ctx'}, dimensions={0}, use_global_device_ids=true | all-gather | bytes 228096 | tf_op jit(solution)/shard_map/all_gather | solution.py:187
  60.1 38.4 %all-gather.2 = bf16[32,1,3456]{2,1,0:T(2,128)(2,1)S(1)} all-gather(bf16[1,1,3456]{2,1,0:T(2,128)(2,1)} %bitcast.262), channel_id=1, replica_groups=mesh['ctx'=32] {'ctx'}, dimensions={0}, use_global_device_ids=true | all-gather | bytes 228096 | tf_op jit(solution)/shard_map/all_gather | solution.py:188
  104.1 42.2 %all-gather.1 = bf16[32,1,10368]{2,1,0:T(2,128)(2,1)S(1)} all-gather(bf16[1,1,10368]{2,1,0:T(2,128)(2,1)S(1)} %bitcast.259), channel_id=1, replica_groups=mesh['ctx'=32] {'ctx'}, dimensions={0}, use_global_device_ids=true | all-gather | bytes 684288 | tf_op jit(solution)/shard_map/all_gather | solution.py:186
  152.0 42.9 %all-gather.3 = bf16[32,1,10368]{2,1,0:T(2,128)(2,1)S(1)} all-gather(bf16[1,1,10368]{2,1,0:T(2,128)(2,1)S(1)} %bitcast.260), channel_id=1, replica_groups=mesh['ctx'=32] {'ctx'}, dimensions={0}, use_global_device_ids=true | all-gather | bytes 684288 | tf_op jit(solution)/shard_map/all_gather | solution.py:189
  207.3 34.2 %while.28 = (s32[]{:T(128)}, f32[3,3,128,64]{2,3,1,0:T(8,128)S(1)}, f32[3,3,128]{2,1,0:T(4,128)S(1)}, f32[3,3,128]{2,1,0:T(4,128)S(1)}, s32[128]{0:T(128)S(1)}, ...) while((s32[]{:T(128)}, f32[3,3,128,64]{2,3,1,0:T(8,128)S(1)}, ...), condition=%wide.region_7.8_spmd.clone, body=%wide.region_4.7_spmd.clone.sunk | while | flops 635664000 | bytes 72688816 | solution.py:87
  210.2 5.3 fusion.138
  215.5 6.1 fusion.139
  227.3 5.3 fusion.138
  232.6 6.1 fusion.139
  244.1 33.5 %reduce.4 = bf16[32,27648]{1,0:T(8,128)(2,1)} reduce(bf16[32,1,27648]{2,1,0:T(2,128)(2,1)} %all-gather.17.cloned.1.call-done, bf16[]{:T(256)} %constant.138), dimensions={1}, to_apply=%all-gather.4.reduce_sub_computation | reduce | bytes 3538946 | tf_op jit(solution)/shard_map/all_gather | solution.py:190
  281.5 6.4 all-gather.19.cloned.1.call-done
  287.9 33.3 %reduce.5 = bf16[32,27648]{1,0:T(8,128)(2,1)} reduce(bf16[32,1,27648]{2,1,0:T(2,128)(2,1)} %all-gather.19.cloned.1.call-done, bf16[]{:T(256)} %constant.138), dimensions={1}, to_apply=%all-gather.5.reduce_sub_computation | reduce | bytes 3538946 | tf_op jit(solution)/shard_map/all_gather | solution.py:191
  329.0 20.5 %all-gather.21.cloned.1.call-done = bf16[32,1,27648]{2,1,0:T(2,128)(2,1)} async-done(((bf16[1,1,27648]{2,1,0:T(2,128)(2,1)}), bf16[32,1,27648]{2,1,0:T(2,128)(2,1)}) %all-gather.21.cloned.1.call-update) | async-done | bytes 1769488 | tf_op jit(solution)/shard_map/all_gather | solution.py:192
  349.5 33.3 %reduce.6 = bf16[32,27648]{1,0:T(8,128)(2,1)} reduce(bf16[32,1,27648]{2,1,0:T(2,128)(2,1)} %all-gather.21.cloned.1.call-done, bf16[]{:T(256)} %constant.138), dimensions={1}, to_apply=%all-gather.6.reduce_sub_computation | reduce | bytes 3538946 | tf_op jit(solution)/shard_map/all_gather | solution.py:192
  397.9 77.7 %while.29 = (s32[]{:T(128)}, f32[3,3,128,64]{2,3,1,0:T(8,128)}, f32[4096,384]{0,1:T(8,128)}, s32[128]{0:T(128)S(1)}, s32[2,2048]{1,0:T(2,128)S(1)}, /*index=5*/s...) while((s32[]{:T(128)}, f32[3,3,128,64]{2,3,1,0:T(8,128)}, ...), condition=%wide.region_12.13_spmd.clone, body=%wide.region_11.12_spmd.clone.sunk | while | flops 1535729664 | bytes 117635888 | solution.py:87
  402.6 5.8 fusion.153
  412.4 5.7 fusion.155
  422.5 15.0 %dynamic_update_slice.5 = f32[4096,384]{0,1:T(8,128)} dynamic-update-slice(f32[4096,384]{0,1:T(8,128)} %get-tuple-element.660, f32[2048,384]{0,1:T(8,128)S(1)} %pad_maximum_fusion.4, s32[]{:T(128)S(6)} %select_n.146, s32[]{:T(128)} %constant.90.clone.1..sunk.1) | dynamic-update-slice | bytes 6291460 | tf_op jit(solution)/shard_map/while/body/eval_jaxpr/dynamic_update_slice | solution.py:287
  441.8 5.7 fusion.153
  451.6 5.7 fusion.155
  461.7 13.8 %dynamic_update_slice.5 = f32[4096,384]{0,1:T(8,128)} dynamic-update-slice(f32[4096,384]{0,1:T(8,128)} %get-tuple-element.660, f32[2048,384]{0,1:T(8,128)S(1)} %pad_maximum_fusion.4, s32[]{:T(128)S(6)} %select_n.146, s32[]{:T(128)} %constant.90.clone.1..sunk.1) | dynamic-update-slice | bytes 6291460 | tf_op jit(solution)/shard_map/while/body/eval_jaxpr/dynamic_update_slice | solution.py:287
  499.5 89.6 %reduce-scatter.2.cloned.1.call-done = f32[128,384]{0,1:T(8,128)} async-done(((f32[4096,384]{0,1:T(8,128)}), f32[128,384]{0,1:T(8,128)}) %reduce-scatter.2.cloned.1.call-update) | async-done | bytes 196624 | tf_op jit(solution)/shard_map/reduce_scatter | solution.py:295
  599.1 41.8 %all-reduce.7 = (f32[576]{0:T(1024)}, f32[576]{0:T(1024)}) all-reduce(f32[576]{0:T(1024)S(1)} %get-tuple-element.331, f32[576]{0:T(1024)S(1)} %copy-done.42), channel_id=1, replica_groups=mesh['ctx'=32] {'ctx'}, use_global_device_ids=true, to_apply=%region_16.17 | all-reduce | flops 1152 | bytes 9216 | tf_op jit(solution)/shard_map/psum | solution.py:334
  641.7 209.3 %all-reduce.11.cloned.1.call-done = (f32[32,10368]{1,0:T(8,128)}, f32[32,3456]{1,0:T(8,128)}, f32[32,3456]{1,0:T(8,128)}, f32[32,10368]{1,0:T(8,128)}, f32[32,27...) async-done(((f32[32,10368]{1,0:T(8,128)}, f32[32,3456]{1,0:T(8,128)}, f32[32,3456]{1,0:T(8,128)}, f32[32,10368]{1,0:T(8,128)}, f32[32,27648]{1,0:T(8,128)}, ...) | async-done | bytes 14155792
  (249 shorter events, 140.3 us)
Async XLA Ops:
  7.2 92.9 %copy-start.4 = (bf16[128,576]{0,1:T(8,128)(2,1)S(1)}, bf16[128,576]{0,1:T(8,128)(2,1)}, u32[]{:S(2)}) copy-start(bf16[128,576]{0,1:T(8,128)(2,1)} %param.17) | copy-start | bytes 442372
  7.2 92.9 %copy-start.31 = (f32[576]{0:T(1024)S(1)}, f32[576]{0:T(1024)}, u32[]{:S(2)}) copy-start(f32[576]{0:T(1024)} %param.18) | copy-start | bytes 6916
  7.2 96.9 %copy-start.36 = (bf16[1,10368]{1,0:T(2,128)(2,1)S(1)}, bf16[1,10368]{1,0:T(2,128)(2,1)}, u32[]{:S(2)}) copy-start(bf16[1,10368]{1,0:T(2,128)(2,1)} %param.19) | copy-start | bytes 62212
  7.2 194.5 %all-gather.13.cloned.1.call-start = ((), (), s32[]{:S(2)}) async-start(), calls=%async_computation.1 | async-start | bytes 1622016 | tf_op jit(solution)/shard_map/all_gather | solution.py:215
  54.2 49.8 %copy-start.15 = (bf16[576,192]{1,0:T(8,128)(2,1)}, bf16[576,192]{1,0:T(8,128)(2,1)S(1)}, u32[]{:S(2)}) copy-start(bf16[576,192]{1,0:T(8,128)(2,1)S(1)} %reshape.311) | copy-start | bytes 663556
  55.4 96.0 %copy-start.39 = (f32[128]{0:T(128)}, f32[128]{0:T(128)S(1)}, u32[]{:S(2)}) copy-start(f32[128]{0:T(128)S(1)} %add_rsqrt_fusion.1) | copy-start | bytes 1540
  58.1 93.8 %copy-start.29 = (f32[128,32]{0,1:T(8,128)}, f32[128,32]{0,1:T(8,128)S(1)}, u32[]{:S(2)}) copy-start(f32[128,32]{0,1:T(8,128)S(1)} %get-tuple-element.419) | copy-start | bytes 49156
  60.1 144.4 %all-gather.15.cloned.1.call-start = ((), (), s32[]{:S(2)}) async-start(), calls=%async_computation.2 | async-start | bytes 1622016 | tf_op jit(solution)/shard_map/all_gather | solution.py:216
  101.1 143.0 %all-gather.17.cloned.1.call-start = ((), (), s32[]{:S(2)}) async-start(), calls=%async_computation.4 | async-start | bytes 3649536 | tf_op jit(solution)/shard_map/all_gather | solution.py:190
  101.9 186.0 %all-gather.19.cloned.1.call-start = ((), (), s32[]{:S(2)}) async-start(), calls=%async_computation.5 | async-start | bytes 3649536 | tf_op jit(solution)/shard_map/all_gather | solution.py:191
  102.4 247.0 %all-gather.21.cloned.1.call-start = ((), (), s32[]{:S(2)}) async-start(), calls=%async_computation.6 | async-start | bytes 3649536 | tf_op jit(solution)/shard_map/all_gather | solution.py:192
  103.0 486.1 %reduce-scatter.2.cloned.1.call-start = ((), (), s32[]{:S(2)}) async-start(), calls=%async_computation.3 | async-start | bytes 6488064 | tf_op jit(solution)/shard_map/reduce_scatter | solution.py:295
  151.1 50.6 %copy-start.9 = (bf16[576,576]{1,0:T(8,128)(2,1)}, bf16[576,576]{1,0:T(8,128)(2,1)S(1)}, u32[]{:S(2)}) copy-start(bf16[576,576]{1,0:T(8,128)(2,1)S(1)} %reshape.313) | copy-start | bytes 1990660
  207.3 36.6 %copy-start.38 = (f32[576]{0:T(1024)S(1)}, f32[576]{0:T(1024)}, u32[]{:S(2)}) copy-start(f32[576]{0:T(1024)} %param.23) | copy-start | bytes 6916
  243.7 148.6 %copy-start.7 = (f32[128,576]{0,1:T(8,128)}, f32[128,576]{0,1:T(8,128)S(1)}, u32[]{:S(2)}) copy-start(f32[128,576]{0,1:T(8,128)S(1)} %get-tuple-element.421) | copy-start | bytes 884740
  244.1 83.5 %copy-start.14 = (bf16[128,576]{0,1:T(8,128)(2,1)}, bf16[128,576]{0,1:T(8,128)(2,1)S(1)}, u32[]{:S(2)}) copy-start(bf16[128,576]{0,1:T(8,128)(2,1)S(1)} %multiply_convert_fusion.3) | copy-start | bytes 442372
  329.0 57.6 %copy-start.26 = (bf16[128,576]{0,1:T(8,128)(2,1)S(1)}, bf16[128,576]{0,1:T(8,128)(2,1)}, u32[]{:S(2)}) copy-start(bf16[128,576]{0,1:T(8,128)(2,1)} %param.29) | copy-start | bytes 442372
  447.5 9.8 %slice-start = ((s8[4718592]{0:T(1024)(128)(4,1)}), s8[4194304]{0:T(1024)(128)(4,1)S(1)}, s32[]{:S(2)}) async-start(s8[4718592]{0:T(1024)(128)(4,1)} %bitcast.225), calls=%async_computation.8 | async-start | bytes 8388608 | tf_op jit(solution)/shard_map/while
  475.6 375.3 %all-reduce.11.cloned.1.call-start = ((), (), s32[]{:S(2)}) async-start(), calls=%async_computation.7 | async-start | bytes 28311552
  495.0 95.0 %copy-start.35 = (f32[128,32]{0,1:T(8,128)S(1)}, f32[128,32]{0,1:T(8,128)}, u32[]{:S(2)}) copy-start(f32[128,32]{0,1:T(8,128)} %get-tuple-element.417) | copy-start | bytes 49156
  495.0 95.1 %copy-start.5 = (bf16[128,576]{0,1:T(8,128)(2,1)S(1)}, bf16[128,576]{0,1:T(8,128)(2,1)}, u32[]{:S(2)}) copy-start(bf16[128,576]{0,1:T(8,128)(2,1)} %param.17) | copy-start | bytes 442372
  495.0 95.1 %copy-start.33 = (f32[576]{0:T(1024)S(1)}, f32[576]{0:T(1024)}, u32[]{:S(2)}) copy-start(f32[576]{0:T(1024)} %param.18) | copy-start | bytes 6916
  495.0 95.1 %copy-start.41 = (f32[128]{0:T(128)S(1)}, f32[128]{0:T(128)}, u32[]{:S(2)}) copy-start(f32[128]{0:T(128)} %copy-done.39) | copy-start | bytes 1540
  593.6 47.3 %copy-start.13 = (f32[128,576]{0,1:T(8,128)S(1)}, f32[128,576]{0,1:T(8,128)}, u32[]{:S(2)}) copy-start(f32[128,576]{0,1:T(8,128)} %copy-done.11) | copy-start | bytes 884740
  (32 other events, 121.3 us)
Sparse Core Ops, SparseCore 0:
  60.2 48.7 all-gather.12
  112.4 49.4 all-gather.14
  164.8 61.3 all-gather.16
  229.0 58.8 all-gather.18
  290.6 58.8 all-gather.20
  475.7 113.3 reduce-scatter.1
  596.7 254.2 all-reduce.10
where the time goes:
time: 880 us; the launch traced here: 870 us
  waiting for transfers between devices  328 us (37%)
  blocking collectives  210 us (24%)
  other arithmetic  139 us (16%)
  local copies, waits for them, and re-layouts  95.2 us (11%)
  matrix products  78.6 us (9%)
  between operations  15 us (2%)
    unnamed x8, waiting for transfers between devices  211 us
    reduce_scatter x1, waiting for transfers between devices, body(): lax.psum_scatter(partial_kv, 'ctx', scatter_dimension=0, tiled=True)  89.6 us
    all_gather x1, blocking collectives, body(): lax.all_gather(key_weight, 'ctx', axis=0, tiled=True)  44.7 us
    all_gather x1, blocking collectives, body(): lax.all_gather(output_weight, 'ctx', axis=0, tiled=True)  42.9 us
    all_gather x1, blocking collectives, body(): lax.all_gather(query_weight, 'ctx', axis=0, tiled=True)  42.2 us
    psum x1, blocking collectives, body(): gain_one, gain_two = lax.psum((first_gain_part, second_gain_part), 'ctx')  41.8 us
    all_gather x1, blocking collectives, body(): lax.all_gather(value_weight, 'ctx', axis=0, tiled=True)  38.4 us
    all_gather x1, other arithmetic, body(): lax.all_gather(gate_weight, 'ctx', axis=0, tiled=True)  33.5 us
  transfers between devices with their start and end apart: 7, of which 4 were waited for; matrix products, arithmetic and copies ran while one was open for 19% of the time, Pallas kernels for 0%

commit v1 on v0

v1 whole, which is shorter than its diff:
```python
import functools

import jax
import jax.numpy as jnp
import numpy as np
from jax import lax
from jax.experimental import pallas as pl
from jax.experimental.pallas import tpu as pltpu
from jax.sharding import PartitionSpec as P

HEADS = 9
KV_HEADS = 3
GROUP = HEADS // KV_HEADS
HEAD_SIZE = 64
KV_WIDTH = KV_HEADS * HEAD_SIZE
TILE = 16

epsilon = 1e-05
rope_base = 100000.0
masked_score = -1e30

low = jnp.bfloat16
full = jnp.float32


def exchange_steps(device_count, low_bits):
    top = device_count.bit_length() - 1
    steps = []
    if low_bits == 0 and top >= 4:
        for bit in range(top - 1, 2, -1):
            steps.append([i ^ (1 << bit) for i in range(device_count)])
        steps.append([i ^ (4 if i & 1 else 2) for i in range(device_count)])
        steps.append([i ^ (2 if i & 1 else 4) for i in range(device_count)])
        steps.append([i ^ 1 for i in range(device_count)])
    else:
        for bit in range(top - 1, low_bits - 1, -1):
            steps.append([i ^ (1 << bit) for i in range(device_count)])
    return steps


def source_table(device_count, low_bits):
    held = [[d >> low_bits] for d in range(device_count)]
    for partner in exchange_steps(device_count, low_bits):
        held = [held[d] + held[partner[d]] for d in range(device_count)]
    return np.array(held, np.int32)


def send(values, partner):
    return lax.ppermute(values, "ctx", [(i, p) for i, p in enumerate(partner)])


def gather_halves(values, steps):
    for partner in steps[:-1]:
        values = jnp.concatenate([values, send(values, partner)], axis=0)
    return values, send(values, steps[-1])


def whole_rows(flat, device, low_bits, columns):
    for bit in range(low_bits):
        partner = [i ^ (1 << bit) for i in range(lax.axis_size("ctx"))]
        other = send(flat, partner)
        is_high = (device >> bit) & 1
        flat = jnp.concatenate(
            [jnp.where(is_high, other, flat), jnp.where(is_high, flat, other)], axis=1
        )
    return flat.reshape(-1, columns)


def own_piece(rows, device, low_bits):
    flat = rows.reshape(1, -1)
    for bit in range(low_bits - 1, -1, -1):
        partner = [i ^ (1 << bit) for i in range(lax.axis_size("ctx"))]
        half = flat.shape[1] // 2
        is_high = (device >> bit) & 1
        leaving = jnp.where(is_high, flat[:, :half], flat[:, half:]).astype(low)
        staying = jnp.where(is_high, flat[:, half:], flat[:, :half])
        flat = staying + send(leaving, partner).astype(full)
    return flat


def low_bits_of(piece, columns):
    low_bits = 0
    while (piece << low_bits) < TILE * columns:
        low_bits += 1
    return low_bits


def fold_rows(rows):
    return jnp.concatenate([rows[:TILE], rows[TILE:].reshape(TILE, -1)], axis=1)


def unfold_rows(packed, columns, folded):
    return jnp.concatenate(
        [packed[:, :columns], packed[:, columns : columns + folded].reshape(-1, columns)], axis=0
    )


def whole_lanes(columns):
    return -(-columns // 128) * 128


def pad_lanes(rows):
    return jnp.pad(rows, ((0, 0), (0, whole_lanes(rows.shape[1]) - rows.shape[1])))


def dot(left, right):
    return jnp.dot(left, right, preferred_element_type=full)


def dot_right(left, right):
    return lax.dot_general(left, right, (((1,), (1,)), ((), ())), preferred_element_type=full)


def dot_left(left, right):
    return lax.dot_general(left, right, (((0,), (0,)), ((), ())), preferred_element_type=full)


def iota(shape, axis):
    return lax.broadcasted_iota(jnp.int32, shape, axis)


def mixing_of(feature_ref):
    width = feature_ref.shape[1]
    return (iota((width, width), 0) == feature_ref[...]).astype(full).astype(low)


def fold_pick(rest, main, fold, at):
    row = iota((rest, main), 0)
    per = TILE // fold
    place = (row // per) * TILE + lax.rem(row, per) * fold + at
    return (iota((rest, main), 1) == place).astype(full).astype(low)


def as_row(column):
    return jnp.transpose(jnp.broadcast_to(column, (column.shape[0], 128)))[0:1]


def turn(values, rope, direction):
    half_dim = HEAD_SIZE // 2
    swapped = jnp.concatenate([values[:, half_dim:], values[:, :half_dim]], axis=1)
    return values * rope[:, :HEAD_SIZE] + swapped * (direction * rope[:, HEAD_SIZE:])


def unit_rows(values):
    inverse = lax.rsqrt(jnp.mean(values * values, axis=-1, keepdims=True) + epsilon)
    return values * inverse, inverse


def norm_back(unit, inverse, gain, grad):
    scaled = grad * gain
    return inverse * (scaled - unit * jnp.mean(scaled * unit, axis=-1, keepdims=True))


def query_range(own, rows, axis):
    shape = (rows, 1) if axis == 0 else (1, rows)
    per_head = rows // GROUP
    half = per_head // 2
    row = lax.rem(iota(shape, axis), per_head)
    first = row < half
    last_key = jnp.where(first, own[0] * half + row, own[1] * half + row - half)
    first_key = jnp.where(first, own[2] * half, own[3] * half)
    return first_key.astype(full), last_key.astype(full)


def gains_block(gains):
    high = gains.astype(low).astype(full)
    return jnp.concatenate([high, gains - high], axis=0).astype(low)


def gains_of(block):
    block = block.astype(full)
    return block[:8] + block[8:]


class Call:
    def __init__(self, steps):
        self.steps = steps

    def spec(self, kind, shape):
        if kind == "smem":
            return pl.BlockSpec(memory_space=pltpu.SMEM)
        if self.steps == 1 or kind == "whole":
            return pl.BlockSpec(memory_space=pltpu.VMEM)
        rest = tuple(shape[1:])
        return pl.BlockSpec((shape[0] // self.steps,) + rest, lambda i: (i,) + (0,) * len(rest))

    def __call__(self, kernel, name, ins, outs, scratch, flops, transcendentals=0):
        steps = self.steps

        def run(*refs):
            kernel(pl.program_id(0) if steps > 1 else 0, steps, *refs)

        size = sum(a.size * a.dtype.itemsize for _, a in ins)
        size += sum(np.prod(s.shape) * s.dtype.itemsize for _, s in outs)
        return pl.pallas_call(
            run,
            grid=(steps,) if steps > 1 else (),
            in_specs=[self.spec(kind, a.shape) for kind, a in ins],
            out_specs=[self.spec(kind, s.shape) for kind, s in outs],
            out_shape=[s for _, s in outs],
            scratch_shapes=scratch,
            compiler_params=pltpu.CompilerParams(vmem_limit_bytes=48 * 1024 * 1024),
            cost_estimate=pl.CostEstimate(
                flops=int(flops), bytes_accessed=int(size), transcendentals=int(transcendentals)
            ),
            name=name,
        )(*[a for _, a in ins])


def once(step, steps, at, action):
    if steps == 1:
        action()
    else:
        pl.when(step == at)(action)


def shape_of(shape, dtype):
    return jax.ShapeDtypeStruct(shape, dtype)


def pack_kernel(merged, step, steps, hidden_ref, gain_ref, *rest):
    packed_ref, normed_ref = rest[-2:]
    width = hidden_ref.shape[1]
    unit, _ = unit_rows(hidden_ref[...].astype(full))
    normed_ref[...] = (unit * gain_ref[...]).astype(low)
    groups = hidden_ref.shape[0] // TILE
    for a in range(groups):
        packed_ref[:, a * width : (a + 1) * width] = normed_ref[a * TILE : (a + 1) * TILE, :]
    if merged:
        packed_ref[:, groups * width :] = rest[0][...]


def project_kernel(
    merged, step, steps, feature_ref, normed_ref, rope_ref, rope_own_ref, own_ref, come_ref, *rest
):
    if merged:
        w_own, w_come = own_ref, come_ref
    else:
        w_own, w_come = rest[:2]
        rest = rest[2:]
    query_ref, kv_own_ref, kv_come_ref, weight_ref, mixed = rest
    width = feature_ref.shape[1]
    groups = rope_own_ref.shape[0] // TILE
    base = groups * width if merged else 0
    columns = weight_ref.shape[1]
    half = w_own.shape[0]
    main = 2 * half
    fold = TILE * main // (TILE * (width - main))

    def first():
        mixed[:half, :] = w_own[:, base : base + columns]
        mixed[half:main, :] = w_come[:, base : base + columns]
        part = columns // fold
        folded = slice(base + columns, base + columns + part)
        extra = jnp.concatenate([w_own[:, folded], w_come[:, folded]], axis=0)
        for at in range(fold):
            mixed[main:, at * part : (at + 1) * part] = dot(
                fold_pick(width - main, main, fold, at), extra
            ).astype(low)
        weight_ref[...] = dot(mixing_of(feature_ref), mixed[...]).astype(low)
        queries = dot(normed_ref[...], weight_ref[:, :width])
        rows = normed_ref.shape[0]
        rope = rope_own_ref[...]
        for head in range(HEADS):
            turned = turn(queries[:, head * HEAD_SIZE : (head + 1) * HEAD_SIZE], rope, 1.0)
            turned = turned.astype(low) * low(HEAD_SIZE**-0.5)
            g = head % GROUP
            query_ref[head // GROUP, g * rows : (g + 1) * rows, :] = turned

    once(step, steps, 0, first)
    rows = own_ref.shape[0]
    for a in range(groups):
        normed = jnp.concatenate(
            [own_ref[:, a * width : (a + 1) * width], come_ref[:, a * width : (a + 1) * width]],
            axis=0,
        )
        kv = dot(normed, weight_ref[:, width:])
        rope = rope_ref[a]
        parts = [
            turn(kv[:, head * HEAD_SIZE : (head + 1) * HEAD_SIZE], rope, 1.0)
            for head in range(KV_HEADS)
        ]
        kv = jnp.concatenate(parts + [kv[:, KV_WIDTH:]], axis=1).astype(low)
        kv_own_ref[:, a * 2 * KV_WIDTH : (a + 1) * 2 * KV_WIDTH] = kv[:rows]
        kv_come_ref[:, a * 2 * KV_WIDTH : (a + 1) * 2 * KV_WIDTH] = kv[rows:]


def key_loop(key_ref, kv_own_ref, kv_come_ref, body):
    groups = kv_own_ref.shape[1] // (2 * KV_WIDTH)
    wide = 4 * KV_WIDTH

    def advance(pair, carry):
        lanes = pl.ds(pl.multiple_of(pair * wide, 128), wide)
        own = kv_own_ref[:, lanes]
        come = kv_come_ref[:, lanes]

        def part(c):
            low_at, high_at = c * HEAD_SIZE, 2 * KV_WIDTH + c * HEAD_SIZE
            return jnp.concatenate(
                [
                    own[:, low_at : low_at + HEAD_SIZE],
                    come[:, low_at : low_at + HEAD_SIZE],
                    own[:, high_at : high_at + HEAD_SIZE],
                    come[:, high_at : high_at + HEAD_SIZE],
                ],
                axis=0,
            )

        start = key_ref[pair // (groups // 4)]
        shift = (lax.rem(pair, groups // 4) * (2 * TILE)).astype(full)
        key_index = jnp.concatenate([start + shift, start + (shift + TILE)], axis=1)
        body(pair, key_index, part)
        return carry

    lax.fori_loop(0, groups // 2, advance, 0)


def forward_kernel(
    step, steps, own, key_ref, query_ref, kv_own_ref, kv_come_ref, out_ref, lse_ref, acc, peak, total
):
    rows = query_ref.shape[1]

    def first():
        acc[...] = jnp.zeros_like(acc)
        peak[...] = jnp.full_like(peak, masked_score)
        total[...] = jnp.zeros_like(total)

    once(step, steps, 0, first)
    first_key, last_key = query_range(own, rows, 0)

    def block(pair, key_index, part):
        allowed = (key_index >= first_key) & (key_index <= last_key)
        for head in range(KV_HEADS):
            scores = dot_right(query_ref[head], part(head))
            masked = jnp.where(allowed, scores, masked_score)
            old = peak[head]
            new = jnp.maximum(old, jnp.max(masked, axis=1, keepdims=True))
            weights = jnp.where(allowed, jnp.exp(masked - new), 0.0)
            factor = jnp.exp(old - new)
            peak[head] = new
            total[head] = total[head] * factor + jnp.sum(weights, axis=1, keepdims=True)
            acc[head] = acc[head] * factor + dot(weights.astype(low), part(KV_HEADS + head))

    key_loop(key_ref, kv_own_ref, kv_come_ref, block)

    def last():
        for head in range(KV_HEADS):
            out_ref[head] = acc[head] / total[head]
            lse_ref[head] = as_row(peak[head] + jnp.log(total[head]))

    once(step, steps, steps - 1, last)


def feedforward_kernel(
    step,
    steps,
    source_ref,
    feature_ref,
    attention_ref,
    hidden_ref,
    gain_ref,
    grad_ref,
    own_ref,
    come_ref,
    out_ref,
    grad_middle_ref,
    head_grad_ref,
    delta_ref,
    keep_ref,
    send_ref,
    gain_part_ref,
    attended,
    output_w,
    normed,
    normed_t,
    down_w,
    down_grad,
    total,
    grad_normed,
    extra_grad,
):
    rows, width = hidden_ref.shape
    half = own_ref.shape[0]
    main = 2 * half
    rest = width - main
    fold = main // rest
    places = main // TILE
    ff = down_w.shape[0]
    chunk = 2 * ff // fold
    down_at = 2 * ff + chunk
    device_ff = ff // places
    groups = device_ff // TILE
    out_at = down_at + groups * width
    mixing = mixing_of(feature_ref)

    for h in range(HEADS):
        g = h % GROUP
        attended[:, h * HEAD_SIZE : (h + 1) * HEAD_SIZE] = attention_ref[
            h // GROUP, g * rows : (g + 1) * rows, :
        ].astype(low)
    attended[...] = dot(attended[...], mixing).astype(low)
    output_w[:half, :] = own_ref[:, out_at : out_at + width]
    output_w[half:main, :] = come_ref[:, out_at : out_at + width]
    part = width // fold
    folded = slice(out_at + width, out_at + width + part)
    extra = jnp.concatenate([own_ref[:, folded], come_ref[:, folded]], axis=0)
    for at in range(fold):
        output_w[main:, at * part : (at + 1) * part] = dot(
            fold_pick(rest, main, fold, at), extra
        ).astype(low)
    middle = hidden_ref[...].astype(full) + dot(attended[...], output_w[...])
    gain = gain_ref[...]
    unit, inverse = unit_rows(middle)
    mixed_norm = dot((unit * gain).astype(low), mixing)
    normed[...] = mixed_norm.astype(low)
    normed_t[...] = jnp.transpose(mixed_norm).astype(low)
    for place in range(places):
        held = own_ref if place < places // 2 else come_ref
        row = (place % (places // 2)) * TILE
        for a in range(groups):
            at = pl.multiple_of(source_ref[place] * device_ff + a * TILE, TILE)
            lane = down_at + a * width
            down_w[pl.ds(at, TILE), :] = held[row : row + TILE, lane : lane + width]
    total[...] = jnp.zeros_like(total)
    grad_normed[...] = jnp.zeros_like(grad_normed)
    extra_grad[...] = jnp.zeros_like(extra_grad)
    out_grad = grad_ref[...]

    def advance(c, carry):
        gate_at = pl.ds(pl.multiple_of(c * chunk, 128), chunk)
        up_at = pl.ds(pl.multiple_of(ff + c * chunk, 128), chunk)
        extra = jnp.concatenate(
            [own_ref[:, 2 * ff : down_at], come_ref[:, 2 * ff : down_at]], axis=0
        )

        def columns(lanes, at):
            pick = fold_pick(rest, main, fold, at)
            tail = dot(pick, extra).astype(low)
            value = (
                dot(normed[:, :half], own_ref[:, lanes])
                + dot(normed[:, half:main], come_ref[:, lanes])
                + dot(normed[:, main:], tail)
            )
            return value, tail, pick

        gate, gate_tail, gate_pick = columns(gate_at, c)
        up, up_tail, up_pick = columns(up_at, c + fold // 2)
        down_at_c = pl.ds(pl.multiple_of(c * chunk, 128), chunk)
        down = down_w[down_at_c, :]
        sigma = 1.0 / (1.0 + jnp.exp(-gate))
        silu = gate * sigma
        inner = (silu * up).astype(low)
        total[...] += dot(inner, down)
        grad_inner = dot_right(out_grad, down)
        grad_gate = (grad_inner * up * sigma * (1.0 + gate * (1.0 - sigma))).astype(low)
        grad_up = (grad_inner * silu).astype(low)
        down_grad[down_at_c, :] = dot_left(inner, out_grad).astype(low)
        for grad, lanes, tail, pick in (
            (grad_gate, gate_at, gate_tail, gate_pick),
            (grad_up, up_at, up_tail, up_pick),
        ):
            grad_normed[:, :half] += dot_right(grad, own_ref[:, lanes])
            grad_normed[:, half:main] += dot_right(grad, come_ref[:, lanes])
            grad_normed[:, main:] += dot_right(grad, tail)
            keep_ref[:, lanes] = dot(normed_t[:half], grad).astype(low)
            send_ref[:, lanes] = dot(normed_t[half:main], grad).astype(low)
            extra_grad[...] += dot_left(pick, dot(normed_t[main:], grad).astype(low))
        return carry

    lax.fori_loop(0, ff // chunk, advance, 0)
    out_ref[...] = (middle + total[...]).astype(low)
    keep_ref[:, 2 * ff : down_at] = extra_grad[:half].astype(low)
    send_ref[:, 2 * ff : down_at] = extra_grad[half:].astype(low)
    for place in range(places):
        held = keep_ref if place < places // 2 else send_ref
        row = (place % (places // 2)) * TILE
        for a in range(groups):
            at = pl.multiple_of(source_ref[place] * device_ff + a * TILE, TILE)
            lane = down_at + a * width
            held[row : row + TILE, lane : lane + width] = down_grad[pl.ds(at, TILE), :]

    high = grad_normed[...].astype(low)
    tail = (grad_normed[...] - high.astype(full)).astype(low)
    back = dot_right(high, mixing) + dot_right(tail, mixing)
    gain_part_ref[...] = jnp.sum(back * unit, axis=0, keepdims=True)
    grad_middle = out_grad.astype(full) + norm_back(unit, inverse, gain, back)
    grad_middle_ref[...] = grad_middle
    grad_branch = grad_middle.astype(low)
    output_grad = dot_left(attended[...], grad_branch).astype(low)
    keep_ref[:, out_at : out_at + width] = output_grad[:half]
    send_ref[:, out_at : out_at + width] = output_grad[half:main]
    extra = sum(
        dot_left(
            fold_pick(rest, main, fold, at), output_grad[main:, at * part : (at + 1) * part]
        )
        for at in range(fold)
    ).astype(low)
    unused = jnp.zeros((half, keep_ref.shape[1] - folded.stop), low)
    for held, rows_of_half in ((keep_ref, extra[:half]), (send_ref, extra[half:])):
        held[:, folded] = rows_of_half
        held[:, folded.stop :] = unused
    grad_low = dot_right(grad_branch, output_w[...]).astype(low)
    grad_low = dot_right(grad_low, mixing).astype(low)
    for kv_head in range(KV_HEADS):
        parts = []
        for g in range(GROUP):
            h = kv_head * GROUP + g
            parts.append(grad_low[:, h * HEAD_SIZE : (h + 1) * HEAD_SIZE])
        grads = jnp.concatenate(parts, axis=0)
        head_grad_ref[kv_head] = grads
        delta_ref[kv_head] = as_row(
            jnp.sum(grads.astype(full) * attention_ref[kv_head], axis=1, keepdims=True)
        )


def backward_kernel(
    merged,
    step,
    steps,
    own,
    feature_ref,
    key_ref,
    query_ref,
    grad_ref,
    lse_ref,
    delta_ref,
    kv_own_ref,
    kv_come_ref,
    own_ref,
    come_ref,
    rope_ref,
    rope_own_ref,
    normed_ref,
    weight_ref,
    gain_ref,
    gain_two_ref,
    query_grad_ref,
    gains_ref,
    *rest,
):
    if merged:
        keep_ref, send_ref = rest[:2]
        w_keep, w_send = keep_ref, send_ref
        rest = rest[2:]
    else:
        keep_ref, send_ref, w_keep, w_send = rest[:4]
        rest = rest[4:]
    grad_query, grad_weight = rest
    rows = query_ref.shape[1]
    tokens, width = normed_ref.shape
    groups = tokens // TILE
    half = own_ref.shape[0]
    base = groups * 2 * KV_WIDTH if merged else 0

    def first():
        grad_query[...] = jnp.zeros_like(grad_query)
        grad_weight[...] = jnp.zeros_like(grad_weight)

    once(step, steps, 0, first)
    first_key, last_key = query_range(own, rows, 1)

    def block(pair, key_index, part):
        key_index = jnp.transpose(jnp.broadcast_to(key_index, (128, key_index.shape[1])))[:, 0:1]
        allowed = (key_index >= first_key) & (key_index <= last_key)
        grad_keys, grad_values = [], []
        for head in range(KV_HEADS):
            keys = part(head)
            scores = dot_right(keys, query_ref[head])
            probs = jnp.where(allowed, jnp.exp(scores - lse_ref[head]), 0.0)
            d_probs = dot_right(part(KV_HEADS + head), grad_ref[head])
            d_scores = (probs * (d_probs - delta_ref[head])).astype(low)
            grad_query[head] += dot_left(keys, d_scores)
            grad_keys.append(dot(d_scores, query_ref[head]))
            grad_values.append(dot(probs.astype(low), grad_ref[head]))
        for i in range(2):
            at = slice(i * 2 * half, (i + 1) * 2 * half)
            rope = rope_ref[2 * pair + i]
            turned = jnp.concatenate(
                [turn(part_of[at], rope, -1.0) for part_of in grad_keys]
                + [part_of[at] for part_of in grad_values],
                axis=1,
            ).astype(low)
            lanes = pl.ds(pl.multiple_of((2 * pair + i) * 2 * KV_WIDTH, 128), 2 * KV_WIDTH)
            keep_ref[:, lanes] = turned[:half]
            send_ref[:half, lanes] = turned[half:]
        lanes = pl.ds(pl.multiple_of(pair * 2 * width, 128), 2 * width)
        n_own = own_ref[:, lanes]
        n_come = come_ref[:, lanes]
        for i in range(2):
            cat = slice(i * width, (i + 1) * width)
            kv_lanes = pl.ds(pl.multiple_of((2 * pair + i) * 2 * KV_WIDTH, 128), 2 * KV_WIDTH)
            grad_weight[:, width:] += dot_left(n_own[:, cat], keep_ref[:, kv_lanes])
            grad_weight[:, width:] += dot_left(n_come[:, cat], send_ref[:half, kv_lanes])

    key_loop(key_ref, kv_own_ref, kv_come_ref, block)

    def last():
        rope = rope_own_ref[...]
        for kv_head in range(KV_HEADS):
            rotated = jnp.transpose(grad_query[kv_head]) * HEAD_SIZE**-0.5
            for g in range(GROUP):
                h = kv_head * GROUP + g
                query_grad_ref[:, h * HEAD_SIZE : (h + 1) * HEAD_SIZE] = turn(
                    rotated[g * tokens : (g + 1) * tokens], rope, -1.0
                ).astype(low)
        grad_weight[:, :width] = dot_left(normed_ref[...], query_grad_ref[...])
        natural = grad_weight[...]
        products = natural * weight_ref[...].astype(full)
        gain_part = as_row(jnp.sum(products, axis=1, keepdims=True)) / gain_ref[...]
        pad = jnp.zeros((8, width), full)
        row = iota((8, width), 0)
        gains = jnp.where(row == 0, gain_part, jnp.where(row == 1, gain_two_ref[...], pad))
        gains_ref[...] = gains
        mixed = dot_left(mixing_of(feature_ref), natural.astype(low)).astype(low)
        columns = mixed.shape[1]
        w_rows = w_keep.shape[0]
        main = 2 * w_rows
        fold = main // (width - main)
        part = columns // fold
        extra = sum(
            dot_left(
                fold_pick(width - main, main, fold, at), mixed[main:, at * part : (at + 1) * part]
            )
            for at in range(fold)
        ).astype(low)
        w_keep[:, base : base + columns] = mixed[:w_rows]
        w_send[:w_rows, base : base + columns] = mixed[w_rows:main]
        folded = slice(base + columns, base + columns + part)
        unused = jnp.zeros((w_rows, w_keep.shape[1] - folded.stop), low)
        w_keep[:, folded] = extra[:w_rows]
        w_send[:w_rows, folded] = extra[w_rows:]
        w_keep[:, folded.stop :] = unused
        w_send[:w_rows, folded.stop :] = unused
        if merged:
            send_ref[half:, :width] = gains_block(gains)
            send_ref[half:, width:] = jnp.zeros((TILE, send_ref.shape[1] - width), low)

    once(step, steps, steps - 1, last)


def add_kernel(with_gains, step, steps, keep_ref, come_ref, *rest):
    rows = keep_ref.shape[0]
    if with_gains:
        gains_ref, rest = rest[0], rest[1:]
        rest, gains_out = rest[:-1], rest[-1]
        width = gains_ref.shape[1]
        gains = gains_of(gains_block(gains_ref[...])) + gains_of(come_ref[rows:, :width])
        gains_out[...] = gains

    def tile(at):
        at = pl.ds(at, TILE)
        return keep_ref[at, :].astype(full) + come_ref[at, :].astype(full)

    if rows == TILE:
        rest[0][...] = tile(0)
        return
    keep_out, send_out = rest
    half = rows // 2

    def advance(i, carry):
        at = pl.multiple_of(i * TILE, TILE)
        keep_out[pl.ds(at, TILE), :] = tile(at).astype(low)
        send_out[pl.ds(at, TILE), :] = tile(pl.multiple_of(half + at, TILE)).astype(low)
        return carry

    lax.fori_loop(0, half // TILE, advance, 0)
    if with_gains:
        send_out[half:, :width] = gains_block(gains)
        send_out[half:, width:] = jnp.zeros((TILE, send_out.shape[1] - width), low)


def scatter_halves(keep, leaving, steps, name, gains=None):
    with_gains = gains is not None
    more = TILE if with_gains else 0
    for partner in reversed(steps):
        come = send(leaving, partner)
        rows, columns = keep.shape
        ins = [("whole", keep), ("whole", come)]
        if rows == TILE:
            outs = [("whole", shape_of((rows, columns), full))]
        else:
            outs = [
                ("whole", shape_of((rows // 2, columns), low)),
                ("whole", shape_of((rows // 2 + more, columns), low)),
            ]
        if with_gains:
            ins.append(("whole", gains))
            outs.append(("whole", shape_of(gains.shape, full)))
        result = Call(1)(functools.partial(add_kernel, with_gains), name, ins, outs, [], 0)
        if with_gains:
            gains = result[-1]
        if rows == TILE:
            return result[0], gains
        keep, leaving = result[0], result[1]


def final_kernel(
    step,
    steps,
    sum_ref,
    query_grad_ref,
    weight_ref,
    hidden_ref,
    gain_ref,
    grad_middle_ref,
    rope_ref,
    out_ref,
    grads,
):
    tokens, width = hidden_ref.shape
    grads[:, :width] = query_grad_ref[...]
    for a in range(tokens // TILE):
        rows = slice(a * TILE, (a + 1) * TILE)
        lanes = slice(a * 2 * KV_WIDTH, (a + 1) * 2 * KV_WIDTH)
        grads[rows, width:] = sum_ref[:, lanes].astype(low)
    back = dot_right(grads[...], weight_ref[...])
    unit, inverse = unit_rows(hidden_ref[...].astype(full))
    out_ref[...] = (grad_middle_ref[...] + norm_back(unit, inverse, gain_ref[...], back)).astype(low)


def body(
    hidden_in,
    attention_gain,
    query_weight,
    key_weight,
    value_weight,
    output_weight,
    feedforward_gain,
    gate_weight,
    up_weight,
    down_weight,
    doc_of_block,
    pair_table,
    out_grad,
):
    tokens, width = hidden_in.shape
    half_rows = tokens // 2
    count = lax.axis_size("ctx")
    device = lax.axis_index("ctx")
    ff = gate_weight.shape[1] * count // width
    low_bits = low_bits_of(query_weight.shape[1], width)
    merged = low_bits == 0
    row_steps = exchange_steps(count, low_bits)
    token_steps = exchange_steps(count, 0)
    group_count = count >> low_bits
    group_rows = width // group_count
    groups = tokens // TILE
    steps = max(1, TILE * count // 512)
    places = count // (2 * steps)
    gain_one = attention_gain.reshape(1, width)
    gain_two = feedforward_gain.reshape(1, width)
    columns = width + 2 * KV_WIDTH

    def rows_of(piece, piece_columns):
        return whole_rows(piece, device, low_bits, piece_columns)

    qkv_piece = pad_lanes(
        fold_rows(
            jnp.concatenate(
                [
                    rows_of(query_weight, width),
                    rows_of(key_weight, KV_WIDTH),
                    rows_of(value_weight, KV_WIDTH),
                ],
                axis=1,
            )
        )
    )
    packed, normed = Call(1)(
        functools.partial(pack_kernel, merged),
        "norm_and_pack",
        [("whole", hidden_in), ("whole", gain_one)] + ([("whole", qkv_piece)] if merged else []),
        [
            (
                "whole",
                shape_of((TILE, groups * width + (qkv_piece.shape[1] if merged else 0)), low),
            ),
            ("whole", shape_of((tokens, width), low)),
        ],
        [],
        0,
    )
    token_halves = gather_halves(packed, token_steps)
    qkv_halves = [] if merged else list(gather_halves(qkv_piece, row_steps))
    down_rows = rows_of(down_weight, width)
    late_piece = pad_lanes(jnp.concatenate(
        [
            fold_rows(jnp.concatenate([rows_of(gate_weight, ff), rows_of(up_weight, ff)], axis=1))
        ]
        + [down_rows[a : a + TILE] for a in range(0, down_rows.shape[0], TILE)]
        + [fold_rows(rows_of(output_weight, width))],
        axis=1,
    ))
    late_halves = gather_halves(late_piece, row_steps)

    def table_row(table):
        return lax.dynamic_index_in_dim(jnp.asarray(table), device, 0, keepdims=False)

    sources = table_row(source_table(count, 0))
    group_table = source_table(count, low_bits)
    group_sources = table_row(group_table)
    inside = np.arange(group_rows)[None, None, :]
    features = group_table[:, :, None] * group_rows + inside
    features = np.concatenate(
        [
            features[:, :, :TILE].reshape(count, -1),
            features[:, :, TILE:].reshape(count, -1),
        ],
        axis=1,
    ).astype(np.int32)
    feature_row = table_row(features).reshape(1, width)

    device_iota = jnp.arange(count, dtype=jnp.int32)
    pairs = jnp.sum(
        jnp.where(sources[:, None] == device_iota[None, :], pair_table[None, :], 0), axis=1
    )
    blocks = jnp.stack([pairs, 2 * count - 1 - pairs], axis=1).reshape(-1)
    block_iota = jnp.arange(2 * count, dtype=jnp.int32)
    block_docs = jnp.sum(
        jnp.where(blocks[:, None] == block_iota[None, :], doc_of_block[None, :], 0), axis=1
    )
    doc_start = jnp.min(
        jnp.where(block_docs[:, None] == doc_of_block[None, :], block_iota[None, :], 2 * count),
        axis=1,
    )
    own = jnp.concatenate([blocks[:2], doc_start[:2]])

    def by_step(values):
        return values.reshape(2, steps, places, 2).transpose(1, 3, 0, 2)

    inner = jnp.arange(TILE, dtype=jnp.int32)
    key_index = by_step(blocks)[..., None] * half_rows + inner
    key_index = key_index.astype(full).reshape(2 * steps, 1, -1)
    frequency = rope_base ** (-jnp.arange(HEAD_SIZE // 2, dtype=full) * (2.0 / HEAD_SIZE))
    block_angle = (by_step(blocks - doc_start) * half_rows).astype(full)[..., None] * frequency
    offset = jnp.arange(half_rows, dtype=full).reshape(groups // 2, TILE)
    offset_angle = offset[..., None] * frequency
    cos_in, sin_in = jnp.cos(offset_angle), jnp.sin(offset_angle)
    times_cos = jnp.concatenate([cos_in, cos_in, -sin_in, sin_in], axis=-1)
    times_sin = jnp.concatenate([sin_in, sin_in, cos_in, -cos_in], axis=-1)
    block_cos = jnp.tile(jnp.cos(block_angle), 4)[:, :, None, :, :, None, :]
    block_sin = jnp.tile(jnp.sin(block_angle), 4)[:, :, None, :, :, None, :]
    rope = (
        block_cos * times_cos[None, None, :, None, None, :, :]
        - block_sin * times_sin[None, None, :, None, None, :, :]
    ).reshape(steps * groups, 2 * places * TILE, 2 * HEAD_SIZE)
    rope_own = rope[:groups, :TILE].reshape(tokens, 2 * HEAD_SIZE)

    call = Call(steps)
    rows = GROUP * tokens
    half = TILE * count // 2
    kv_shape = shape_of((half, groups * 2 * KV_WIDTH), low)
    head_shape = (KV_HEADS, rows, HEAD_SIZE)
    key_total = TILE * count * groups
    queries, kv_own, kv_come, qkv_weight = call(
        functools.partial(project_kernel, merged),
        "project",
        [
            ("whole", feature_row),
            ("whole", normed),
            ("rows", rope),
            ("whole", rope_own),
            ("rows", token_halves[0]),
            ("rows", token_halves[1]),
        ]
        + [("whole", a) for a in qkv_halves],
        [
            ("whole", shape_of(head_shape, low)),
            ("rows", kv_shape),
            ("rows", kv_shape),
            ("whole", shape_of((width, columns), low)),
        ],
        [pltpu.VMEM((width, columns), low)],
        2 * key_total * width * 2 * KV_WIDTH,
    )
    attention, lse = call(
        forward_kernel,
        "attention_forward",
        [
            ("smem", own),
            ("rows", key_index),
            ("whole", queries),
            ("rows", kv_own),
            ("rows", kv_come),
        ],
        [
            ("whole", shape_of(head_shape, full)),
            ("whole", shape_of((KV_HEADS, 1, rows), full)),
        ],
        [
            pltpu.VMEM(head_shape, full),
            pltpu.VMEM((KV_HEADS, rows, 1), full),
            pltpu.VMEM((KV_HEADS, rows, 1), full),
        ],
        4 * KV_HEADS * rows * key_total * HEAD_SIZE,
        KV_HEADS * rows * key_total,
    )
    late_shape = late_halves[0].shape
    main = 2 * late_shape[0]
    block_out, grad_middle, head_grads, delta, late_keep, late_send, gain_two_part = Call(1)(
        feedforward_kernel,
        "feedforward",
        [
            ("smem", group_sources),
            ("whole", feature_row),
            ("whole", attention),
            ("whole", hidden_in),
            ("whole", gain_two),
            ("whole", out_grad),
            ("whole", late_halves[0]),
            ("whole", late_halves[1]),
        ],
        [
            ("whole", shape_of((tokens, width), low)),
            ("whole", shape_of((tokens, width), full)),
            ("whole", shape_of(head_shape, low)),
            ("whole", shape_of((KV_HEADS, 1, rows), full)),
            ("whole", shape_of(late_shape, low)),
            ("whole", shape_of(late_shape, low)),
            ("whole", shape_of((1, width), full)),
        ],
        [
            pltpu.VMEM((tokens, width), low),
            pltpu.VMEM((width, width), low),
            pltpu.VMEM((tokens, width), low),
            pltpu.VMEM((width, tokens), low),
            pltpu.VMEM((ff, width), low),
            pltpu.VMEM((ff, width), low),
            pltpu.VMEM((tokens, width), full),
            pltpu.VMEM((tokens, width), full),
            pltpu.VMEM((main, 2 * ff * (width - main) // main), full),
        ],
        6 * tokens * width * (3 * ff + width),
        tokens * ff,
    )
    late_sum, _ = scatter_halves(late_keep, late_send, row_steps, "add_late")

    w_folded = columns * (width - main) // main
    w_columns = whole_lanes(columns + w_folded)
    if merged:
        chain = [
            ("whole", shape_of((half, kv_shape.shape[1] + w_columns), low)),
            ("whole", shape_of((half + TILE, kv_shape.shape[1] + w_columns), low)),
        ]
    else:
        chain = [("rows", kv_shape), ("rows", kv_shape)]
        chain += [("whole", shape_of((main // 2, w_columns), low))] * 2
    query_grad, gains, *chain = call(
        functools.partial(backward_kernel, merged),
        "attention_backward",
        [
            ("smem", own),
            ("whole", feature_row),
            ("rows", key_index),
            ("whole", queries),
            ("whole", head_grads),
            ("whole", lse),
            ("whole", delta),
            ("rows", kv_own),
            ("rows", kv_come),
            ("rows", token_halves[0]),
            ("rows", token_halves[1]),
            ("rows", rope),
            ("whole", rope_own),
            ("whole", normed),
            ("whole", qkv_weight),
            ("whole", gain_one),
            ("whole", gain_two_part),
        ],
        [("whole", shape_of((tokens, width), low)), ("whole", shape_of((8, width), full))] + chain,
        [
            pltpu.VMEM((KV_HEADS, HEAD_SIZE, rows), full),
            pltpu.VMEM((width, columns), full),
        ],
        10 * KV_HEADS * rows * key_total * HEAD_SIZE + 2 * key_total * width * 2 * KV_WIDTH,
        KV_HEADS * rows * key_total,
    )
    if merged:
        own_sum, gains = scatter_halves(chain[0], chain[1], token_steps, "add_chain", gains)
        kv_sum, qkv_sum = own_sum, own_sum[:, kv_shape.shape[1] :]
    else:
        kv_sum, _ = scatter_halves(chain[0], chain[1], token_steps, "add_kv")
        qkv_sum, _ = scatter_halves(chain[2], chain[3], row_steps, "add_qkv")
        gains = lax.psum(gains, "ctx")
    (input_grad,) = Call(1)(
        final_kernel,
        "input_gradient",
        [
            ("whole", kv_sum),
            ("whole", query_grad),
            ("whole", qkv_weight),
            ("whole", hidden_in),
            ("whole", gain_one),
            ("whole", grad_middle),
            ("whole", rope_own),
        ],
        [("whole", shape_of((tokens, width), low))],
        [pltpu.VMEM((tokens, columns), low)],
        2 * tokens * width * columns,
    )

    def piece_of(rows):
        return own_piece(rows, device, low_bits)

    qkv_rows = unfold_rows(qkv_sum, columns, w_folded)
    ff_folded = 2 * ff * (width - main) // main
    down_at = 2 * ff + ff_folded
    ff_rows = unfold_rows(late_sum, 2 * ff, ff_folded)
    device_groups = ff // group_count // TILE
    out_at = down_at + device_groups * width
    down_rows = jnp.concatenate(
        [late_sum[:, down_at + a * width : down_at + (a + 1) * width] for a in range(device_groups)],
        axis=0,
    )
    output_rows = unfold_rows(late_sum[:, out_at:], width, width * (width - main) // main)
    return (
        block_out,
        input_grad,
        gains[0],
        piece_of(qkv_rows[:, :width]),
        piece_of(qkv_rows[:, width : width + KV_WIDTH]),
        piece_of(qkv_rows[:, width + KV_WIDTH :]),
        piece_of(output_rows),
        gains[1],
        piece_of(ff_rows[:, :ff]),
        piece_of(ff_rows[:, ff:]),
        piece_of(down_rows),
    )


def solution(mesh):
    row = P("ctx", None)
    in_specs = (row, P(), row, row, row, row, P(), row, row, row, P(), P(), row)
    out_specs = (row, row, P(), row, row, row, row, P(), row, row, row)
    return jax.shard_map(body, mesh=mesh, in_specs=in_specs, out_specs=out_specs, check_vma=False)
```

time: 880 us -> 258 us (0.29); the launches traced: 870 us -> 257 us
  waiting for transfers between devices: 328 us -> 114 us
  blocking collectives: 210 us -> 0 us
  other arithmetic: 139 us -> 7.08 us
  Pallas kernels: 0 us -> 78.9 us
  matrix products: 78.6 us -> 0 us
  local copies, waits for them, and re-layouts: 95.2 us -> 28.1 us
  starting transfers between devices: 0.28 us -> 28.3 us
  between operations: 15 us -> 1.08 us
    unnamed x8 -> x0, waiting for transfers between devices: 211 us -> none
    all_gather x4 -> x0, blocking collectives: 168 us -> none  [the longest x1 44.7 us: body(): lax.all_gather(key_weight, 'ctx', axis=0, tiled=True)]
    ppermute x0 -> x20, waiting for transfers between devices: none -> 114 us  [send(): return lax.ppermute(values, 'ctx', [(i, p) for i, p in enumerate(partner)])]
    all_gather x7 -> x0, other arithmetic: 111 us -> none  [the longest x1 33.5 us: body(): lax.all_gather(gate_weight, 'ctx', axis=0, tiled=True)]
    reduce_scatter x1 -> x0, waiting for transfers between devices: 89.6 us -> none  [body(): lax.psum_scatter(partial_kv, 'ctx', scatter_dimension=0, tiled=True)]
    pallas_call x0 -> x16, Pallas kernels: none -> 78.9 us  [__call__(): pl.pallas_call(run, grid=(steps,) if steps > 1 else (), in_specs=[self.sp...]
    dot_general x35 -> x0, matrix products: 78.6 us -> none  [the longest x2 11.5 us: backward_terms(): jnp.einsum('fiam,pim->iafp', head_gradient_rows, head_values, preferred_e...]
    psum x1 -> x0, blocking collectives: 41.8 us -> none  [body(): gain_one, gain_two = lax.psum((first_gain_part, second_gain_part), 'ctx')]
  transfers between devices with their start and end apart: 7 -> 20, of which waited for: 4 -> 15; matrix products, arithmetic and copies ran while one was open for 19% -> 9% of each run, Pallas kernels for 0% -> 24%
where the time goes in v1:
time: 258 us; the launch traced here: 257 us
  waiting for transfers between devices  114 us (44%)
  Pallas kernels  78.9 us (31%)
  starting transfers between devices  28.3 us (11%)
  local copies, waits for them, and re-layouts  28.1 us (11%)
  other arithmetic  7.08 us (3%)
    ppermute x20, waiting for transfers between devices, send(): return lax.ppermute(values, 'ctx', [(i, p) for i, p in enumerate(partner)])  114 us
    pallas_call x16, Pallas kernels, __call__(): pl.pallas_call(run, grid=(steps,) if steps > 1 else (), in_specs=[self.sp...  78.9 us
    ppermute x20, starting transfers between devices, send(): return lax.ppermute(values, 'ctx', [(i, p) for i, p in enumerate(partner)])  28.3 us
    unnamed x28, local copies, waits for them, and re-layouts  13.2 us
  transfers between devices with their start and end apart: 20, of which 15 were waited for; matrix products, arithmetic and copies ran while one was open for 9% of the time, Pallas kernels for 24%

profile of v1, /device:TPU:0, one launch (start us, length us, event | category | flops | bytes accessed | tf_op | source)
XLA Modules:
  0.0 257.3 jit_solution(2801965996418353812)
XLA Ops:
  5.6 4.1 %collective-permute-start = (bf16[16,5760]{1,0:T(8,128)(2,1)S(1)}, bf16[16,5760]{1,0:T(8,128)(2,1)S(1)}, u32[]{:S(2)}, u32[]{:S(2)}) collective-permute-start(bf16[16,5760]{1,0:T(8,128)(2,1)S(1)} %get-tuple-element.53), channel_id=1, source_target_pairs={{0,16},{1,17},{2,18},{3,19},{4,20},{5,21},{6,22},{7,23},{8,24},{9,... | collective-permute-start | bytes 552968 | tf_op jit(solution)/shard_map/ppermute | solution.py:49
  18.4 4.9 %collective-permute-start.1 = (bf16[32,5760]{1,0:T(8,128)(2,1)S(1)}, bf16[32,5760]{1,0:T(8,128)(2,1)S(1)}, u32[]{:S(2)}, u32[]{:S(2)}) collective-permute-start(bf16[32,5760]{1,0:T(8,128)(2,1)S(1)} %pad_maximum_fusion.5), channel_id=1, source_target_pairs={{0,8},{1,9},{2,10},{3,11},{4,12},{5,13},{6,14},{7,15},{8,0},{9,1},... | collective-permute-start | bytes 1105928 | tf_op jit(solution)/shard_map/ppermute | solution.py:49
  24.0 3.7 %collective-permute-done.5 = bf16[16,5888]{1,0:T(8,128)(2,1)S(1)} collective-permute-done((bf16[16,5888]{1,0:T(8,128)(2,1)S(1)}, bf16[16,5888]{1,0:T(8,128)(2,1)S(1)}, u32[]{:S(2)}, u32[]{:S(2)}) %collective-permute-start.5) | collective-permute-done | bytes 188448 | tf_op jit(solution)/shard_map/ppermute | solution.py:49
  28.5 7.1 %collective-permute-done.1 = bf16[32,5760]{1,0:T(8,128)(2,1)S(1)} collective-permute-done((bf16[32,5760]{1,0:T(8,128)(2,1)S(1)}, bf16[32,5760]{1,0:T(8,128)(2,1)S(1)}, u32[]{:S(2)}, u32[]{:S(2)}) %collective-permute-start.1) | collective-permute-done | bytes 368672 | tf_op jit(solution)/shard_map/ppermute | solution.py:49
  37.9 5.1 %collective-permute-done.6 = bf16[32,5888]{1,0:T(8,128)(2,1)S(1)} collective-permute-done((bf16[32,5888]{1,0:T(8,128)(2,1)S(1)}, bf16[32,5888]{1,0:T(8,128)(2,1)S(1)}, u32[]{:S(2)}, u32[]{:S(2)}) %collective-permute-start.6) | collective-permute-done | bytes 376864 | tf_op jit(solution)/shard_map/ppermute | solution.py:49
  45.4 1.8 collective-permute-done.2
  48.8 13.6 %collective-permute-done.7 = bf16[64,5888]{1,0:T(8,128)(2,1)S(1)} collective-permute-done((bf16[64,5888]{1,0:T(8,128)(2,1)S(1)}, bf16[64,5888]{1,0:T(8,128)(2,1)S(1)}, u32[]{:S(2)}, u32[]{:S(2)}) %collective-permute-start.7) | collective-permute-done | bytes 753696 | tf_op jit(solution)/shard_map/ppermute | solution.py:49
  66.0 3.0 %collective-permute-done.3 = bf16[128,5760]{1,0:T(8,128)(2,1)S(1)} collective-permute-done((bf16[128,5760]{1,0:T(8,128)(2,1)S(1)}, bf16[128,5760]{1,0:T(8,128)(2,1)S(1)}, u32[]{:S(2)}, u32[]{:S(2)}) %collective-permute-start.3) | collective-permute-done | bytes 1474592 | tf_op jit(solution)/shard_map/ppermute | solution.py:49
  70.2 2.1 collective-permute-start.4
  72.3 12.9 %collective-permute-done.8 = bf16[128,5888]{1,0:T(8,128)(2,1)S(1)} collective-permute-done((bf16[128,5888]{1,0:T(8,128)(2,1)S(1)}, bf16[128,5888]{1,0:T(8,128)(2,1)S(1)}, u32[]{:S(2)}, u32[]{:S(2)}) %collective-permute-start.8) | collective-permute-done | bytes 1507360 | tf_op jit(solution)/shard_map/ppermute | solution.py:49
  86.4 1.8 collective-permute-start.9
  92.2 12.2 %project.1 = (bf16[3,384,64]{2,1,0:T(8,128)(2,1)S(1)}, bf16[256,3072]{1,0:T(8,128)(2,1)S(1)}, bf16[256,3072]{1,0:T(8,128)(2,1)S(1)}, bf16[576,960]{1,0:T(8,128)(2,1)S(1)}) custom-call(s32[1,576]{1,0:T(1,128)S(1)} %constant_dynamic-slice_fusion.refs_0_.refs_1_, bf16[128,576]{1,0:T(8,128)(2,1)S(1)} %get-tuple-element.52.refs_1_.refs_13_, ...), custom_call_target="tpu_custom_call" | custom-call | flops 1811939328 | bytes 12609792 | tf_op jit(solution)/shard_map/project/pallas_call | solution.py:195
  104.4 13.4 %attention_forward.1 = (f32[3,384,64]{2,1,0:T(8,128)S(1)}, f32[3,1,384]{2,1,0:T(1,128)S(1)}) custom-call(s32[4]{0:T(128)S(1)} %pad_add_fusion.3.refs_0_, f32[2,1,512]{2,1,0:T(1,128)S(1)} %add_convert_fusion.refs_1_.refs_2_, bf16[3,384,64]{2,1,0:T(8,128)(2,1)S(1)} %get-tuple-element.54.refs_2_.refs_3_, ...), custom_call_target="tpu_custom_call" | custom-call | flops 1207959552 | bytes 3596816 | tf_op jit(solution)/shard_map/attention_forward/pallas_call | solution.py:195
  117.8 16.9 %feedforward.1 = (bf16[128,576]{1,0:T(8,128)(2,1)S(1)}, f32[128,576]{1,0:T(8,128)S(1)}, bf16[3,384,64]{2,1,0:T(8,128)(2,1)S(1)}, f32[3,1,384]{2,1,0:T(1,128)S(1)...) custom-call(s32[32]{0:T(128)S(1)} %dynamic-slice_bitcast_fusion.refs_0_, ...), custom_call_target="tpu_custom_call" | custom-call | flops 2293235712 | bytes 13249920 | tf_op jit(solution)/shard_map/feedforward/pallas_call | solution.py:195
  134.7 28.8 %attention_backward.1 = (bf16[128,576]{1,0:T(8,128)(2,1)S(1)}, f32[8,576]{1,0:T(8,128)S(1)}, bf16[256,4224]{1,0:T(8,128)(2,1)}, bf16[272,4224]{1,0:T(8,128)(2,1)}) custom-call(s32[4]{0:T(128)S(1)} %pad_add_fusion.3.refs_0_, s32[1,576]{1,0:T(1,128)S(1)} %constant_dynamic-slice_fusion.refs_0_.refs_1_, f32[2,1,512]{2,1,0:T(1,128)S(1)} %add_convert_fusion.refs_1_.refs_2_, ...), custom_call_target="tpu_custom_call" | custom-call | flops 4831838208 | bytes 17401616 | tf_op jit(solution)/shard_map/attention_backward/pallas_call | solution.py:195
  164.1 4.3 %collective-permute-done.10.refs_1_ = bf16[272,4224]{1,0:T(8,128)(2,1)S(1)} collective-permute-done((bf16[272,4224]{1,0:T(8,128)(2,1)}, bf16[272,4224]{1,0:T(8,128)(2,1)S(1)}, u32[]{:S(2)}, u32[]{:S(2)}) %collective-permute-start.10) | collective-permute-done | bytes 2297888 | tf_op jit(solution)/shard_map/ppermute | solution.py:49
  171.3 2.2 add_chain.5
  175.1 2.6 add_late.5
  178.3 11.9 %collective-permute-done.11.refs_1_ = bf16[144,4224]{1,0:T(8,128)(2,1)S(1)} collective-permute-done((bf16[144,4224]{1,0:T(8,128)(2,1)S(1)}, bf16[144,4224]{1,0:T(8,128)(2,1)S(1)}, u32[]{:S(2)}, u32[]{:S(2)}) %collective-permute-start.11) | collective-permute-done | bytes 1216544 | tf_op jit(solution)/shard_map/ppermute | solution.py:49
  192.1 21.6 %collective-permute-done.16.refs_1_ = bf16[128,5888]{1,0:T(8,128)(2,1)S(1)} collective-permute-done((bf16[128,5888]{1,0:T(8,128)(2,1)S(1)}, bf16[128,5888]{1,0:T(8,128)(2,1)S(1)}, u32[]{:S(2)}, u32[]{:S(2)}) %collective-permute-start.16) | collective-permute-done | bytes 1507360 | tf_op jit(solution)/shard_map/ppermute | solution.py:49
  215.8 10.5 %collective-permute-done.13.refs_1_ = bf16[48,4224]{1,0:T(8,128)(2,1)S(1)} collective-permute-done((bf16[48,4224]{1,0:T(8,128)(2,1)S(1)}, bf16[48,4224]{1,0:T(8,128)(2,1)S(1)}, u32[]{:S(2)}, u32[]{:S(2)}) %collective-permute-start.13) | collective-permute-done | bytes 405536 | tf_op jit(solution)/shard_map/ppermute | solution.py:49
  228.7 1.7 collective-permute-start.18
  231.2 8.8 %collective-permute-done.14.refs_1_ = bf16[32,4224]{1,0:T(8,128)(2,1)S(1)} collective-permute-done((bf16[32,4224]{1,0:T(8,128)(2,1)S(1)}, bf16[32,4224]{1,0:T(8,128)(2,1)S(1)}, u32[]{:S(2)}, u32[]{:S(2)}) %collective-permute-start.14) | collective-permute-done | bytes 270368 | tf_op jit(solution)/shard_map/ppermute | solution.py:49
  245.9 8.1 %collective-permute-done.19.refs_1_ = bf16[16,5888]{1,0:T(8,128)(2,1)S(1)} collective-permute-done((bf16[16,5888]{1,0:T(8,128)(2,1)S(1)}, bf16[16,5888]{1,0:T(8,128)(2,1)S(1)}, u32[]{:S(2)}, u32[]{:S(2)}) %collective-permute-start.19) | collective-permute-done | bytes 188448 | tf_op jit(solution)/shard_map/ppermute | solution.py:49
  (153 shorter events, 53.3 us)
Async XLA Ops:
  0.6 17.2 %copy-start.5 = (s32[32]{0:T(128)S(1)}, s32[32]{0:T(128)}, u32[]{:S(2)}) copy-start(s32[32]{0:T(128)} %param.27) | copy-start | bytes 388
  5.6 12.7 %collective-permute-start = (bf16[16,5760]{1,0:T(8,128)(2,1)S(1)}, bf16[16,5760]{1,0:T(8,128)(2,1)S(1)}, u32[]{:S(2)}, u32[]{:S(2)}) collective-permute-start(bf16[16,5760]{1,0:T(8,128)(2,1)S(1)} %get-tuple-element.53), channel_id=1, source_target_pairs={{0,16},{1,17},{2,18},{3,19},{4,20},{5,21},{6,22},{7,23},{8,24},{9,... | collective-permute-start | bytes 552968 | tf_op jit(solution)/shard_map/ppermute | solution.py:49
  16.4 11.2 %collective-permute-start.5 = (bf16[16,5888]{1,0:T(8,128)(2,1)S(1)}, bf16[16,5888]{1,0:T(8,128)(2,1)S(1)}, u32[]{:S(2)}, u32[]{:S(2)}) collective-permute-start(bf16[16,5888]{1,0:T(8,128)(2,1)S(1)} %get-tuple-element.137), channel_id=1, source_target_pairs={{0,16},{1,17},{2,18},{3,19},{4,20},{5,21},{6,22},{7,23},{8,24},{9,... | collective-permute-start | bytes 565256 | tf_op jit(solution)/shard_map/ppermute | solution.py:49
  18.4 17.2 %collective-permute-start.1 = (bf16[32,5760]{1,0:T(8,128)(2,1)S(1)}, bf16[32,5760]{1,0:T(8,128)(2,1)S(1)}, u32[]{:S(2)}, u32[]{:S(2)}) collective-permute-start(bf16[32,5760]{1,0:T(8,128)(2,1)S(1)} %pad_maximum_fusion.5), channel_id=1, source_target_pairs={{0,8},{1,9},{2,10},{3,11},{4,12},{5,13},{6,14},{7,15},{8,0},{9,1},... | collective-permute-start | bytes 1105928 | tf_op jit(solution)/shard_map/ppermute | solution.py:49
  27.7 15.3 %collective-permute-start.6 = (bf16[32,5888]{1,0:T(8,128)(2,1)S(1)}, bf16[32,5888]{1,0:T(8,128)(2,1)S(1)}, u32[]{:S(2)}, u32[]{:S(2)}) collective-permute-start(bf16[32,5888]{1,0:T(8,128)(2,1)S(1)} %pad_maximum_fusion.4), channel_id=1, source_target_pairs={{0,8},{1,9},{2,10},{3,11},{4,12},{5,13},{6,14},{7,15},{8,0},{9,1},... | collective-permute-start | bytes 1130504 | tf_op jit(solution)/shard_map/ppermute | solution.py:49
  35.6 11.5 %collective-permute-start.2 = (bf16[64,5760]{1,0:T(8,128)(2,1)S(1)}, bf16[64,5760]{1,0:T(8,128)(2,1)S(1)}, u32[]{:S(2)}, u32[]{:S(2)}) collective-permute-start(bf16[64,5760]{1,0:T(8,128)(2,1)S(1)} %pad_maximum_fusion.3), channel_id=1, source_target_pairs={{0,2},{1,5},{2,0},{3,7},{4,6},{5,1},{6,4},{7,3},{8,10},{9,13},{10,... | collective-permute-start | bytes 2211848 | tf_op jit(solution)/shard_map/ppermute | solution.py:49
  43.0 19.4 %collective-permute-start.7 = (bf16[64,5888]{1,0:T(8,128)(2,1)S(1)}, bf16[64,5888]{1,0:T(8,128)(2,1)S(1)}, u32[]{:S(2)}, u32[]{:S(2)}) collective-permute-start(bf16[64,5888]{1,0:T(8,128)(2,1)S(1)} %pad_maximum_fusion.2), channel_id=1, source_target_pairs={{0,2},{1,5},{2,0},{3,7},{4,6},{5,1},{6,4},{7,3},{8,10},{9,13},{10,... | collective-permute-start | bytes 2261000 | tf_op jit(solution)/shard_map/ppermute | solution.py:49
  47.3 21.8 %collective-permute-start.3 = (bf16[128,5760]{1,0:T(8,128)(2,1)S(1)}, bf16[128,5760]{1,0:T(8,128)(2,1)S(1)}, u32[]{:S(2)}, u32[]{:S(2)}) collective-permute-start(bf16[128,5760]{1,0:T(8,128)(2,1)S(1)} %pad_maximum_fusion.1), channel_id=1, source_target_pairs={{0,4},{1,3},{2,6},{3,1},{4,0},{5,7},{6,2},{7,5},{8,12},{9,11},{10,... | collective-permute-start | bytes 4423688 | tf_op jit(solution)/shard_map/ppermute | solution.py:49
  62.5 22.6 %collective-permute-start.8 = (bf16[128,5888]{1,0:T(8,128)(2,1)S(1)}, bf16[128,5888]{1,0:T(8,128)(2,1)S(1)}, u32[]{:S(2)}, u32[]{:S(2)}) collective-permute-start(bf16[128,5888]{1,0:T(8,128)(2,1)S(1)} %pad_maximum_fusion), channel_id=1, source_target_pairs={{0,4},{1,3},{2,6},{3,1},{4,0},{5,7},{6,2},{7,5},{8,12},{9,11},{10,... | collective-permute-start | bytes 4521992 | tf_op jit(solution)/shard_map/ppermute | solution.py:49
  66.0 22.4 %copy-start.4 = (f32[576]{0:T(1024)S(1)}, f32[576]{0:T(1024)}, u32[]{:S(2)}) copy-start(f32[576]{0:T(1024)} %param.22) | copy-start | bytes 6916
  66.0 22.6 %copy-start.6 = (s32[64]{0:T(128)S(1)}, s32[64]{0:T(128)}, u32[]{:S(2)}) copy-start(s32[64]{0:T(128)} %param.26) | copy-start | bytes 772
  66.0 24.0 %copy-start.3 = (bf16[128,576]{0,1:T(8,128)(2,1)S(1)}, bf16[128,576]{0,1:T(8,128)(2,1)}, u32[]{:S(2)}) copy-start(bf16[128,576]{0,1:T(8,128)(2,1)} %param.28) | copy-start | bytes 442372
  70.2 21.6 %collective-permute-start.4 = (bf16[256,5760]{1,0:T(8,128)(2,1)}, bf16[256,5760]{1,0:T(8,128)(2,1)}, u32[]{:S(2)}, u32[]{:S(2)}) collective-permute-start(bf16[256,5760]{1,0:T(8,128)(2,1)} %constant_dynamic-update-slice_fusion.refs_4_.refs_9_), channel_id=1, source_target_pairs={{0,1},{1,0},{2,3},{3,2},{4,5},{5,4},{6,7},{7,6},{8,9},{9,8},{10,11... | collective-permute-start | bytes 8847368 | tf_op jit(solution)/shard_map/ppermute | solution.py:49
  86.4 31.4 %collective-permute-start.9 = (bf16[256,5888]{1,0:T(8,128)(2,1)}, bf16[256,5888]{1,0:T(8,128)(2,1)}, u32[]{:S(2)}, u32[]{:S(2)}) collective-permute-start(bf16[256,5888]{1,0:T(8,128)(2,1)} %constant_dynamic-update-slice_fusion.7.refs_6_), channel_id=1, source_target_pairs={{0,1},{1,0},{2,3},{3,2},{4,5},{5,4},{6,7},{7,6},{8,9},{9,8},{10,11... | collective-permute-start | bytes 9043976 | tf_op jit(solution)/shard_map/ppermute | solution.py:49
  134.7 40.4 %collective-permute-start.15 = (bf16[256,5888]{1,0:T(8,128)(2,1)}, bf16[256,5888]{1,0:T(8,128)(2,1)}, u32[]{:S(2)}, u32[]{:S(2)}) collective-permute-start(bf16[256,5888]{1,0:T(8,128)(2,1)} %get-tuple-element.84), channel_id=1, source_target_pairs={{0,1},{1,0},{2,3},{3,2},{4,5},{5,4},{6,7},{7,6},{8,9},{9,8},{10,11... | collective-permute-start | bytes 9043976 | tf_op jit(solution)/shard_map/ppermute | solution.py:49
  163.5 4.8 %collective-permute-start.10 = (bf16[272,4224]{1,0:T(8,128)(2,1)}, bf16[272,4224]{1,0:T(8,128)(2,1)S(1)}, u32[]{:S(2)}, u32[]{:S(2)}) collective-permute-start(bf16[272,4224]{1,0:T(8,128)(2,1)} %get-tuple-element.65), channel_id=1, source_target_pairs={{0,1},{1,0},{2,3},{3,2},{4,5},{5,4},{6,7},{7,6},{8,9},{9,8},{10,11... | collective-permute-start | bytes 6893576 | tf_op jit(solution)/shard_map/ppermute | solution.py:49
  173.6 16.7 %collective-permute-start.11 = (bf16[144,4224]{1,0:T(8,128)(2,1)S(1)}, bf16[144,4224]{1,0:T(8,128)(2,1)S(1)}, u32[]{:S(2)}, u32[]{:S(2)}) collective-permute-start(bf16[144,4224]{1,0:T(8,128)(2,1)S(1)} %get-tuple-element.68), channel_id=1, source_target_pairs={{0,4},{1,3},{2,6},{3,1},{4,0},{5,7},{6,2},{7,5},{8,12},{9,11},{10,... | collective-permute-start | bytes 3649544 | tf_op jit(solution)/shard_map/ppermute | solution.py:49
  177.7 35.9 %collective-permute-start.16 = (bf16[128,5888]{1,0:T(8,128)(2,1)S(1)}, bf16[128,5888]{1,0:T(8,128)(2,1)S(1)}, u32[]{:S(2)}, u32[]{:S(2)}) collective-permute-start(bf16[128,5888]{1,0:T(8,128)(2,1)S(1)} %get-tuple-element.86), channel_id=1, source_target_pairs={{0,4},{1,3},{2,6},{3,1},{4,0},{5,7},{6,2},{7,5},{8,12},{9,11},{10,... | collective-permute-start | bytes 4521992 | tf_op jit(solution)/shard_map/ppermute | solution.py:49
  190.5 25.0 %collective-permute-start.12 = (bf16[80,4224]{1,0:T(8,128)(2,1)S(1)}, bf16[80,4224]{1,0:T(8,128)(2,1)S(1)}, u32[]{:S(2)}, u32[]{:S(2)}) collective-permute-start(bf16[80,4224]{1,0:T(8,128)(2,1)S(1)} %get-tuple-element.71), channel_id=1, source_target_pairs={{0,2},{1,5},{2,0},{3,7},{4,6},{5,1},{6,4},{7,3},{8,10},{9,13},{10,... | collective-permute-start | bytes 2027528 | tf_op jit(solution)/shard_map/ppermute | solution.py:49
  214.0 13.8 %collective-permute-start.17 = (bf16[64,5888]{1,0:T(8,128)(2,1)S(1)}, bf16[64,5888]{1,0:T(8,128)(2,1)S(1)}, u32[]{:S(2)}, u32[]{:S(2)}) collective-permute-start(bf16[64,5888]{1,0:T(8,128)(2,1)S(1)} %get-tuple-element.88), channel_id=1, source_target_pairs={{0,2},{1,5},{2,0},{3,7},{4,6},{5,1},{6,4},{7,3},{8,10},{9,13},{10,... | collective-permute-start | bytes 2261000 | tf_op jit(solution)/shard_map/ppermute | solution.py:49
  215.7 10.6 %collective-permute-start.13 = (bf16[48,4224]{1,0:T(8,128)(2,1)S(1)}, bf16[48,4224]{1,0:T(8,128)(2,1)S(1)}, u32[]{:S(2)}, u32[]{:S(2)}) collective-permute-start(bf16[48,4224]{1,0:T(8,128)(2,1)S(1)} %get-tuple-element.74), channel_id=1, source_target_pairs={{0,8},{1,9},{2,10},{3,11},{4,12},{5,13},{6,14},{7,15},{8,0},{9,1},... | collective-permute-start | bytes 1216520 | tf_op jit(solution)/shard_map/ppermute | solution.py:49
  226.4 13.6 %collective-permute-start.14 = (bf16[32,4224]{1,0:T(8,128)(2,1)S(1)}, bf16[32,4224]{1,0:T(8,128)(2,1)S(1)}, u32[]{:S(2)}, u32[]{:S(2)}) collective-permute-start(bf16[32,4224]{1,0:T(8,128)(2,1)S(1)} %get-tuple-element.77), channel_id=1, source_target_pairs={{0,16},{1,17},{2,18},{3,19},{4,20},{5,21},{6,22},{7,23},{8,24},{9,... | collective-permute-start | bytes 811016 | tf_op jit(solution)/shard_map/ppermute | solution.py:49
  228.7 14.9 %collective-permute-start.18 = (bf16[32,5888]{1,0:T(8,128)(2,1)}, bf16[32,5888]{1,0:T(8,128)(2,1)S(1)}, u32[]{:S(2)}, u32[]{:S(2)}) collective-permute-start(bf16[32,5888]{1,0:T(8,128)(2,1)} %get-tuple-element.90), channel_id=1, source_target_pairs={{0,8},{1,9},{2,10},{3,11},{4,12},{5,13},{6,14},{7,15},{8,0},{9,1},... | collective-permute-start | bytes 1130504 | tf_op jit(solution)/shard_map/ppermute | solution.py:49
  243.7 10.2 %collective-permute-start.19 = (bf16[16,5888]{1,0:T(8,128)(2,1)S(1)}, bf16[16,5888]{1,0:T(8,128)(2,1)S(1)}, u32[]{:S(2)}, u32[]{:S(2)}) collective-permute-start(bf16[16,5888]{1,0:T(8,128)(2,1)S(1)} %get-tuple-element.92), channel_id=1, source_target_pairs={{0,16},{1,17},{2,18},{3,19},{4,20},{5,21},{6,22},{7,23},{8,24},{9,... | collective-permute-start | bytes 565256 | tf_op jit(solution)/shard_map/ppermute | solution.py:49
  (3 other events, 4.4 us)
